TPU v7x, 32 devices: a whole 2x2x4 slice. The times are simulated.
32 devices in a mesh: ctx: 16 (over z, y, core), exp: 2 (over x).
Axes of the slice: x: 2, y: 2, z: 4, core: 2. Of those that a mesh axis runs over, the one named last changes fastest.
Arguments:
- queries: bfloat16 [2048, 32, 128], P('ctx', 'exp'), may hold values from -100 to 100
- keys: bfloat16 [2048, 2, 128], P('ctx'), may hold values from -4 to 4
- values: bfloat16 [2048, 2, 128], P('ctx'), may hold values from -4 to 4
- resid: bfloat16 [2048, 4096], P('ctx', 'exp'), may hold values from -20 to 20
- gain: float32 [4096], P('exp'), may hold values from 0.1 to 1.9
- expert_ids: int32 [2048, 8], P('ctx'), may hold values from 0 to 127, all different within a row; in each aligned block of 128 rows (0 to 127, 128 to 255, ...) at most 10 rows name the same one
- gate_scores: float32 [2048, 8], P('ctx'), may hold values from 0.05 to 1
- w_gate_up: bfloat16 [16, 4096, 2, 768], P('ctx', 'exp'), may hold values from -0.09375 to 0.09375
- w_down: bfloat16 [16, 768, 4096], P('ctx', None, 'exp'), may hold values from -0.625 to 0.625
- w_out: bfloat16 [32, 128, 4096], P('exp', 'ctx'), may hold values from -0.5 to 0.5
Outputs:
- context: bfloat16 [2048, 32, 128], P('ctx', 'exp')
- mixed: bfloat16 [2048, 4096], P('ctx', 'exp')
Inputs may be any that keep to these rules, and one draw needn't show every extreme that they name: `expert_ids`: each row names 8 different experts; within the 128 rows of one index of ctx no expert is named more than 10 times.
All inputs are finite; a program needn't handle non-finite values.
Results may differ from a plain program's by a relative error of at most 0.02.
Values may be sent and summed in bfloat16 or wider, within the bound.
A program may use at most 64 MiB of HBM per device.

v0:
```python
import math

import jax
import jax.numpy as jnp
from jax import lax
from jax.sharding import PartitionSpec as P

D = 4096
HQ = 32
KVH = 2
EXPERTS = 128
TOPK = 8


masked_score = -1e30
epsilon = 1e-06


def attend_piece(state_now, pair_piece, offset, query_rows, query_pos, last_pos, scaling):
    key_piece, value_piece = pair_piece
    length = key_piece.shape[0]

    def compute(state_in):
        running, denominator, numerator = state_in
        scores = (
            jnp.einsum("rd,kd->rk", query_rows, key_piece, preferred_element_type=jnp.float32)
            * scaling
        )
        key_pos = jnp.arange(length, dtype=jnp.int32)
        visible = key_pos[None, :] <= query_pos[:, None]
        masked = jnp.where(visible, scores, masked_score)
        highest = jnp.maximum(running, jnp.max(masked, axis=1))
        weights_exp = jnp.where(visible, jnp.exp(masked - highest[:, None]), 0.0)
        rounded = weights_exp.astype(jnp.bfloat16)
        numerator = jnp.dot(rounded, value_piece, preferred_element_type=jnp.float32)
        denominator = jnp.sum(weights_exp, axis=1)
        return (highest, denominator, numerator)

    def untouched(state_in):
        return state_in

    return lax.cond(offset <= last_pos, compute, untouched, state_now)


def body(queries, keys, values, resid, gain, expert_ids, gate_scores, w_gate_up, w_down, w_out):
    tokens_here = queries.shape[0]
    heads_here = queries.shape[1]
    head_size = queries.shape[2]
    ctx_count = lax.axis_size("ctx")
    ctx_place = lax.axis_index("ctx")
    exp_place = lax.axis_index("exp")
    own_pos = ctx_place * tokens_here + jnp.arange(tokens_here, dtype=jnp.int32)
    query_sets = (queries, own_pos)
    group_index = exp_place * heads_here // (HQ // KVH)
    key_local = lax.dynamic_index_in_dim(keys, group_index, 1, keepdims=False)
    value_local = lax.dynamic_index_in_dim(values, group_index, 1, keepdims=False)
    scaling = 1.0 / math.sqrt(head_size)
    set_queries, set_pos = query_sets
    set_rows = set_queries.shape[0] * heads_here
    initial = [
        (
            jnp.full((set_rows,), masked_score, jnp.float32),
            jnp.zeros((set_rows,), jnp.float32),
            jnp.zeros((set_rows, head_size), jnp.float32),
        )
    ]
    rows_set = set_queries.reshape(set_rows, head_size)
    pos_set = jnp.repeat(set_pos, heads_here)
    last_set = jnp.max(set_pos)
    updated = [
        attend_piece(
            tuple(initial)[0],
            (
                lax.all_gather(key_local, "ctx", axis=0, tiled=True),
                lax.all_gather(value_local, "ctx", axis=0, tiled=True),
            ),
            jnp.int32(0),
            rows_set,
            pos_set,
            last_set,
            scaling,
        )
    ]
    folded = tuple(updated)
    pieces_out = []
    for state_set in folded:
        normalized = state_set[2] / state_set[1][:, None]
        pieces_out.append(normalized.reshape(-1, heads_here, head_size).astype(jnp.bfloat16))
    context = pieces_out[0]
    whole_out = lax.all_gather(w_out, "ctx", axis=1, tiled=True)
    projected = jnp.einsum("thp,hpd->td", context, whole_out, preferred_element_type=jnp.float32)
    attended = lax.psum_scatter(
        projected.astype(jnp.bfloat16), "exp", scatter_dimension=1, tiled=True
    ).astype(jnp.float32)
    hidden_state = resid.astype(jnp.float32) + attended
    square_sum = lax.psum(jnp.sum(hidden_state * hidden_state, axis=1), "exp")
    inverse = lax.rsqrt(square_sum / D + epsilon)
    normed = (hidden_state * inverse[:, None] * gain[None, :]).astype(jnp.bfloat16)
    capacity = max(2, 5 * tokens_here * TOPK // (4 * EXPERTS))
    flat_ids = expert_ids.reshape(-1)
    onehot = (flat_ids[:, None] == jnp.arange(ctx_count, dtype=jnp.int32)[None, :]).astype(
        jnp.int32
    )
    earlier = jnp.cumsum(onehot, axis=0) - onehot
    rank_of = jnp.sum(earlier * onehot, axis=1)
    active = flat_ids < ctx_count
    slot_of = jnp.where(active, flat_ids * capacity + rank_of, -1).reshape(tokens_here, TOPK)
    slot_range = jnp.arange(ctx_count * capacity, dtype=jnp.int32)
    dispatch_map = jnp.zeros((ctx_count * capacity, tokens_here), jnp.bfloat16)
    for column in range(TOPK):
        dispatch_map = dispatch_map + (slot_range[:, None] == slot_of[None, :, column]).astype(
            jnp.bfloat16
        )
    local_width = normed.shape[1]
    outgoing = jnp.dot(dispatch_map, normed, preferred_element_type=jnp.float32).astype(
        jnp.bfloat16
    )
    outgoing = outgoing.reshape(ctx_count, capacity, local_width)
    arrived = lax.all_to_all(outgoing, "ctx", split_axis=0, concat_axis=0, tiled=True)
    sources = arrived.shape[0]
    width_slots = arrived.shape[1]
    row_block = arrived.reshape(sources * width_slots, local_width)
    partial_sum = jnp.einsum(
        "rd,dgf->rgf", row_block, w_gate_up[0], preferred_element_type=jnp.float32
    )
    summed = lax.psum(partial_sum.astype(jnp.bfloat16), "exp").astype(jnp.float32)
    hidden_units = (jax.nn.silu(summed[:, 0]) * summed[:, 1]).astype(jnp.bfloat16)
    result = jnp.dot(hidden_units, w_down[0], preferred_element_type=jnp.float32).astype(
        jnp.bfloat16
    )
    result = result.reshape(sources, width_slots, local_width)
    returned = lax.all_to_all(result, "ctx", split_axis=0, concat_axis=0, tiled=True)
    back_rows = returned.reshape(ctx_count * capacity, local_width)
    picked = jnp.take(back_rows, jnp.maximum(slot_of, 0).reshape(-1), axis=0).reshape(
        tokens_here, TOPK, local_width
    )
    weight_now = gate_scores / jnp.sum(gate_scores, axis=1, keepdims=True)
    weight_now = jnp.where(active.reshape(tokens_here, TOPK), weight_now, 0.0)
    routed = jnp.zeros((tokens_here, local_width), jnp.float32)
    for column in range(TOPK):
        routed = routed + weight_now[:, column : column + 1] * picked[:, column].astype(jnp.float32)
    mixed = (hidden_state + routed).astype(jnp.bfloat16)
    return (context, mixed)


def solution(mesh):
    in_specs = (
        P("ctx", "exp", None),
        P("ctx", None, None),
        P("ctx", None, None),
        P("ctx", "exp"),
        P("exp"),
        P("ctx", None),
        P("ctx", None),
        P("ctx", "exp", None, None),
        P("ctx", None, "exp"),
        P("exp", "ctx", None),
    )
    out_specs = (P("ctx", "exp", None), P("ctx", "exp"))
    return jax.shard_map(body, mesh=mesh, in_specs=in_specs, out_specs=out_specs, check_vma=False)
```

profile of v0, /device:TPU:1, one launch (start us, length us, event | category | flops | bytes accessed | tf_op | source)
XLA Modules:
  0.0 312.8 jit_solution(8072603061787061455)
XLA Ops:
  7.2 0.0 copy-start
  7.2 0.0 all-gather.4.cloned.1.call-start
  7.2 0.7 all-gather.4.cloned.1.call-update
  7.9 0.0 reduce-scatter.2.cloned.1.call-start
  8.0 1.0 constant_dynamic-slice_fusion.1
  9.0 0.9 constant_dynamic-slice_fusion
  10.0 0.6 fusion.70
  11.3 27.4 %all-gather = bf16[2048,1,128]{2,0,1:T(8,128)(2,1)} all-gather(bf16[128,1,128]{2,0,1:T(8,128)(2,1)S(1)} %copy.64), channel_id=2, replica_groups=mesh['ctx'=16,'exp'=2] {'ctx'}, dimensions={0}, use_global_device_ids=true | all-gather | bytes 557056 | tf_op jit(solution)/shard_map/all_gather | solution.py:74
  38.7 23.3 %all-gather.1 = bf16[2048,1,128]{2,0,1:T(8,128)(2,1)} all-gather(bf16[128,1,128]{2,0,1:T(8,128)(2,1)S(1)} %copy.65), channel_id=3, replica_groups=mesh['ctx'=16,'exp'=2] {'ctx'}, dimensions={0}, use_global_device_ids=true | all-gather | bytes 557056 | tf_op jit(solution)/shard_map/all_gather | solution.py:75
  62.0 14.9 %conditional.1 = (f32[2048]{0:T(1024)S(1)}, f32[2048,128]{1,0:T(8,128)}) conditional(s32[]{:T(128)} %convert_element_type.124, () %tuple.16, (s32[128]{0:T(128)S(1)}, bf16[128,16,128]{2,1,0:T(8,128)(2,1)}, bf16[2048,128]{1,0:T(8,128)(2,1)}, bf16[2048,128]{1,0:T(8,128)(2,1)}) %tuple.44), branch_computations={%region_1.2_spmd, %region_2.5_spmd} | conditional | flops 2214590464 | bytes 55149100 | solution.py:42
  62.0 0.1 broadcast_in_dim.27
  62.1 0.1 le.24
  62.2 0.0 copy-start.1
  62.2 4.2 %fusion = (f32[2048]{0:T(1024)S(1)}, f32[2048,2048]{0,1:T(8,128)S(1)}) fusion(s32[2048]{0:T(1024)S(1)} %le.24, bf16[2048,128]{1,0:T(8,128)(2,1)} %bitcast.123, bf16[2048,128]{1,0:T(8,128)(2,1)} %get-tuple-element.12), kind=kOutput, calls=%fused_computation.4 | convolution fusion | flops 1090516992 | bytes 17842176 | tf_op jit(solution)/shard_map/cond/branch_1_fun/rd,kd->rk/dot_general | solution.py:26
  66.4 0.0 copy-done.1
  66.4 5.7 %fusion.3 = f32[2048,128]{1,0:T(8,128)} fusion(bf16[2048,128]{1,0:T(8,128)(2,1)S(1)} %copy-done.1, f32[2048,2048]{0,1:T(8,128)S(1)} %get-tuple-element.25, f32[2048]{0:T(1024)S(1)} %broadcast_maximum_fusion, s32[2048]{0:T(1024)S(1)} %le.24), kind=kOutput, calls=%fused_computation.7 | convolution fusion | flops 1098907648 | bytes 18366464 | tf_op jit(solution)/shard_map/cond/branch_1_fun/dot_general | solution.py:35
  72.0 4.9 %fusion.2 = f32[2048]{0:T(1024)S(1)} fusion(f32[2048,2048]{0,1:T(8,128)S(1)} %get-tuple-element.25, f32[2048]{0:T(1024)S(1)} %broadcast_maximum_fusion, s32[2048]{0:T(1024)S(1)} %le.24), kind=kLoop, calls=%fused_computation.6 | loop fusion | flops 25163776 | bytes 16801792 | tf_op jit(solution)/shard_map/cond/branch_1_fun/reduce_sum | solution.py:36
  77.0 0.0 copy-start.2
  77.0 0.0 copy-start.4
  77.0 2.4 divide_convert_fusion
  79.4 64.7 %all-gather.4.cloned.1.call-done = bf16[16,128,4096]{2,1,0:T(8,128)(2,1)} async-done(((bf16[16,8,4096]{2,1,0:T(8,128)(2,1)}), bf16[16,128,4096]{2,1,0:T(8,128)(2,1)}) %all-gather.4.cloned.1.call-update) | async-done | bytes 16777232 | tf_op jit(solution)/shard_map/all_gather | solution.py:90
  144.1 9.3 %fusion.10 = bf16[128,4096]{1,0:T(8,128)(2,1)} fusion(bf16[16,128,4096]{2,1,0:T(8,128)(2,1)} %all-gather.4.cloned.1.call-done, bf16[128,16,128]{2,1,0:T(8,128)(2,1)} %bitcast.115), kind=kOutput, calls=%fused_computation.15 | convolution fusion | flops 2148007936 | bytes 18350080 | tf_op jit(solution)/shard_map/thp,hpd->td/dot_general | solution.py:91
  153.3 0.0 copy-start.3
  153.4 0.0 reduce-scatter.2.cloned.1.call-update
  153.4 0.0 all-reduce.2.cloned.1.call-start
  153.4 0.0 copy-done.2
  153.4 0.1 copy.56
  153.5 0.1 eq.149
  153.6 0.1 eq.145
  153.7 4.5 %reduce-window.6 = s32[16,8,128]{2,1,0:T(8,128)S(1)} reduce-window(s32[16,8,128]{2,1,0:T(8,128)S(1)} %fusion.45, s32[]{:T(128)} %constant.70.clone.1), window={size=1x1x128 pad=0_0x0_0x127_0}, to_apply=%region_7.8 | reduce-window | flops 2080768 | bytes 131076 | tf_op jit(solution)/shard_map/reduce-window
  158.3 0.1 slice.114
  158.3 0.1 copy.58
  158.5 0.1 copy.59
  158.6 0.1 broadcast_add_fusion
  158.7 0.1 reduce_sum.40
  158.9 12.7 %reduce-scatter.2.cloned.1.call-done = bf16[128,2048]{1,0:T(8,128)(2,1)} async-done(((bf16[128,4096]{1,0:T(8,128)(2,1)}), bf16[128,2048]{1,0:T(8,128)(2,1)}) %reduce-scatter.2.cloned.1.call-update) | async-done | bytes 524304 | tf_op jit(solution)/shard_map/reduce_scatter | solution.py:92
  171.6 1.5 multiply_reduce_fusion
  173.0 3.8 %psum.14 = f32[128]{0:T(128)S(1)} all-reduce(f32[128]{0:T(128)S(1)} %multiply_reduce_fusion), channel_id=1, replica_groups=mesh['ctx'=16,'exp'=2] {'exp'}, use_global_device_ids=true, to_apply=%region_11.12 | all-reduce | flops 128 | bytes 1024 | tf_op jit(solution)/shard_map/psum | solution.py:96
  176.8 0.0 copy-done.4
  176.8 2.5 convolution_convert_fusion
  179.4 2.2 reshape.120
  181.5 32.7 %all_to_all.10 = bf16[16,10,2048]{2,1,0:T(8,128)(2,1)} all-to-all(bf16[16,10,2048]{2,1,0:T(8,128)(2,1)} %reshape.120), channel_id=1, replica_groups=mesh['ctx'=16,'exp'=2] {'ctx'}, dimensions={0} | all-to-all | bytes 1310720 | tf_op jit(solution)/shard_map/all_to_all | solution.py:119
  214.2 2.1 reshape.144
  216.4 5.0 %fusion.16 = bf16[160,2,768]{2,0,1:T(8,128)(2,1)} fusion(bf16[160,2048,1]{1,0,2:T(8,128)(2,1)} %reshape.144, bf16[2048,2,768]{2,1,0:T(2,128)(2,1)} %bitcast.122), kind=kOutput, calls=%fused_computation.21 | convolution fusion | flops 1006878720 | bytes 7438336 | tf_op jit(solution)/shard_map/rd,dgf->rgf/dot_general | solution.py:123
  221.4 0.0 all-reduce.2.cloned.1.call-update
  221.4 26.5 %all-reduce.2.cloned.1.call-done = bf16[160,2,768]{2,0,1:T(8,128)(2,1)} async-done(((bf16[160,2,768]{2,0,1:T(8,128)(2,1)}), bf16[160,2,768]{2,0,1:T(8,128)(2,1)}) %all-reduce.2.cloned.1.call-update) | async-done | bytes 491536 | tf_op jit(solution)/shard_map/psum | solution.py:126
  247.9 1.1 convert_element_type.143
  249.0 0.0 copy-done
  249.0 1.6 fusion.13
  250.6 2.2 reshape.122
  252.8 6.2 %all-to-all-start.1 = ((bf16[16,10,2048]{2,1,0:T(8,128)(2,1)}), bf16[16,10,2048]{2,1,0:T(8,128)(2,1)}, u32[]{:S(2)}, u32[]{:S(2)}) async-start(bf16[16,10,2048]{2,1,0:T(8,128)(2,1)} %reshape.122), calls=%async_computation.2 | async-start | bytes 2097152 | tf_op jit(solution)/shard_map/all_to_all | solution.py:132
  259.0 0.1 copy.62
  259.1 0.1 reshape.124
  259.2 0.0 copy-done.3
  259.3 23.0 %all-to-all-done.1 = bf16[16,10,2048]{2,1,0:T(8,128)(2,1)} async-done(((bf16[16,10,2048]{2,1,0:T(8,128)(2,1)}), bf16[16,10,2048]{2,1,0:T(8,128)(2,1)}, u32[]{:S(2)}, u32[]{:S(2)}) %all-to-all-start.1) | async-done | bytes 655392 | tf_op jit(solution)/shard_map/all_to_all | solution.py:132
  282.2 2.2 reshape.123
  284.4 10.0 %gather_fusion = bf16[1024,2048]{1,0:T(8,128)(2,1)} fusion(bf16[160,2048]{1,0:T(8,128)(2,1)} %reshape.123, s32[1024]{0:T(1024)S(1)} %broadcast_clamp_fusion), kind=kCustom, calls=%fused_computation | custom fusion | bytes 8392704 | tf_op jit(solution)/shard_map/jit(_take)/gather | solution.py:134
  294.4 8.8 %copy_select_fusion = bf16[128,8,2048]{2,0,1:T(8,128)(2,1)S(1)} fusion(bf16[128,8,2048]{2,1,0:T(8,128)(2,1)} %bitcast.114, pred[128,8]{0,1:T(8,128)(4,1)S(1)} %get-tuple-element.22), kind=kLoop, calls=%fused_computation.16 | loop fusion | flops 2097152 | bytes 8389632 | tf_op jit(solution)/shard_map/jit(_take)/select_n | solution.py:134
  303.2 3.0 fusion.21
  (18 shorter events, 0.2 us)
Async XLA Ops:
  7.2 241.8 %copy-start = (bf16[1,768,2048]{2,1,0:T(8,128)(2,1)S(1)}, bf16[1,768,2048]{2,1,0:T(8,128)(2,1)}, u32[]{:S(2)}) copy-start(bf16[1,768,2048]{2,1,0:T(8,128)(2,1)} %param.20) | copy-start | bytes 9437188
  7.2 136.9 %all-gather.4.cloned.1.call-start = ((), (), s32[]{:S(2)}) async-start(), calls=%async_computation.3 | async-start | bytes 17825792 | tf_op jit(solution)/shard_map/all_gather | solution.py:90
  7.9 163.7 %reduce-scatter.2.cloned.1.call-start = ((), (), s32[]{:S(2)}) async-start(), calls=%async_computation.4 | async-start | bytes 1572864 | tf_op jit(solution)/shard_map/reduce_scatter | solution.py:92
  62.2 4.2 %copy-start.1 = (bf16[2048,128]{1,0:T(8,128)(2,1)S(1)}, bf16[2048,128]{1,0:T(8,128)(2,1)}, u32[]{:S(2)}) copy-start(bf16[2048,128]{1,0:T(8,128)(2,1)} %get-tuple-element.13) | copy-start | bytes 1572868 | tf_op jit(solution)/shard_map/cond
  77.0 76.5 %copy-start.2 = (s32[128,8]{0,1:T(8,128)S(1)}, s32[128,8]{0,1:T(8,128)}, u32[]{:S(2)}) copy-start(s32[128,8]{0,1:T(8,128)} %param.17) | copy-start | bytes 12292
  77.0 99.9 %copy-start.4 = (f32[2048]{0:T(1024)S(1)}, f32[2048]{0:T(1024)}, u32[]{:S(2)}) copy-start(f32[2048]{0:T(1024)} %param.16) | copy-start | bytes 24580
  153.3 105.8 %copy-start.3 = (f32[128,8]{0,1:T(8,128)S(1)}, f32[128,8]{0,1:T(8,128)}, u32[]{:S(2)}) copy-start(f32[128,8]{0,1:T(8,128)} %param.18) | copy-start | bytes 12292
  153.4 94.5 %all-reduce.2.cloned.1.call-start = ((), (), s32[]{:S(2)}) async-start(), calls=%async_computation.5 | async-start | bytes 983040 | tf_op jit(solution)/shard_map/psum | solution.py:126
  252.8 29.4 %all-to-all-start.1 = ((bf16[16,10,2048]{2,1,0:T(8,128)(2,1)}), bf16[16,10,2048]{2,1,0:T(8,128)(2,1)}, u32[]{:S(2)}, u32[]{:S(2)}) async-start(bf16[16,10,2048]{2,1,0:T(8,128)(2,1)} %reshape.122), calls=%async_computation.2 | async-start | bytes 2097152 | tf_op jit(solution)/shard_map/all_to_all | solution.py:132
Sparse Core Ops, SparseCore 0:
  10.2 133.7 all-gather.3
  153.5 18.0 reduce-scatter.1
  221.5 26.3 all-reduce.1
where the time goes:
time: 314 us; the launch traced here: 313 us
  waiting for transfers between devices  128 us (41%)
  blocking collectives  87.2 us (28%)
  matrix products  28.2 us (9%)
  other arithmetic  27.1 us (9%)
  local copies, waits for them, and re-layouts  21.8 us (7%)
  between operations  14.6 us (5%)
  starting transfers between devices  6.32 us (2%)
    all_gather x1, waiting for transfers between devices, body(): whole_out = lax.all_gather(w_out, 'ctx', axis=1, tiled=True)  64.7 us
    all_to_all x1, blocking collectives, body(): lax.all_to_all(outgoing, 'ctx', split_axis=0, concat_axis=0, tiled=True)  32.7 us
    all_gather x1, blocking collectives, body(): lax.all_gather(key_local, 'ctx', axis=0, tiled=True)  27.4 us
    psum x1, waiting for transfers between devices, body(): lax.psum(partial_sum.astype(jnp.bfloat16), 'exp').astype(jnp.float32)  26.5 us
    all_gather x1, blocking collectives, body(): lax.all_gather(value_local, 'ctx', axis=0, tiled=True)  23.3 us
    all_to_all x1, waiting for transfers between devices, body(): lax.all_to_all(result, 'ctx', split_axis=0, concat_axis=0, tiled=True)  23 us
    reduce_scatter x1, waiting for transfers between devices, body(): lax.psum_scatter(projected.astype(jnp.bfloat16), 'exp', scatter_dimension...  12.7 us
    gather x1, local copies, waits for them, and re-layouts, body(): jnp.take(back_rows, jnp.maximum(slot_of, 0).reshape(-1), axis=0)  10 us
  transfers between devices with their start and end apart: 4, of which 4 were waited for; matrix products, arithmetic and copies ran while one was open for 8% of the time, Pallas kernels for 0%

commit v1 on v0

--- a/solution.py
+++ b/solution.py
@@ -1,8 +1,11 @@
+import functools
 import math
 
 import jax
 import jax.numpy as jnp
 from jax import lax
+from jax.experimental import pallas as pl
+from jax.experimental.pallas import tpu as pltpu
 from jax.sharding import PartitionSpec as P
 
 D = 4096
@@ -42,7 +45,7 @@
     return lax.cond(offset <= last_pos, compute, untouched, state_now)
 
 
-def body(queries, keys, values, resid, gain, expert_ids, gate_scores, w_gate_up, w_down, w_out):
+def general_body(queries, keys, values, resid, gain, expert_ids, gate_scores, w_gate_up, w_down, w_out):
     tokens_here = queries.shape[0]
     heads_here = queries.shape[1]
     head_size = queries.shape[2]
@@ -143,6 +146,447 @@
     return (context, mixed)
 
 
+MESH = pl.DeviceIdType.MESH
+F32 = jnp.float32
+BF16 = jnp.bfloat16
+N_Z = 4
+PLANE = 4
+
+
+def attend_kernel(
+    q_ref, kv_ref, w_hbm, resid_ref, ctx_ref, hid_ref,
+    kvbuf, wbuf, rows32, ctx2d, ctxbuf, target, acc,
+    kv_send, kv_recv, w_up, w_down_sem, w_y, w_sib, w_recv, x_send, c_send, c_recv, local_sem,
+):
+    c = lax.axis_index("ctx")
+    e = lax.axis_index("exp")
+    z = c // PLANE
+    y = (c // 2) % 2
+    k = c % 2
+    plane = c % PLANE
+    y_peer = z * PLANE + (1 - y) * 2 + k
+    sibling = z * PLANE + y * 2 + (1 - k)
+    half = resid_ref.shape[1]
+    tokens = resid_ref.shape[0]
+    heads = q_ref.shape[0] // tokens
+    depth = wbuf.shape[2]
+
+    barrier = pltpu.get_barrier_semaphore()
+    for step in range(1, N_Z):
+        pl.semaphore_signal(
+            barrier, inc=1, device_id=(((z + step) % N_Z) * PLANE + plane, e), device_id_type=MESH
+        )
+    pl.semaphore_signal(barrier, inc=1, device_id=(y_peer, e), device_id_type=MESH)
+    pl.semaphore_signal(barrier, inc=1, device_id=(sibling, e), device_id_type=MESH)
+    pl.semaphore_signal(barrier, inc=1, device_id=(c, 1 - e), device_id_type=MESH)
+    own_w = pltpu.make_async_copy(
+        w_hbm.at[:, pl.ds(pl.multiple_of(e * half, half), half)], wbuf.at[c, e], local_sem.at[0]
+    )
+    own_w.start()
+    kvbuf[c] = kv_ref[...]
+    pl.semaphore_wait(barrier, N_Z + 2)
+
+    def kv_copy(block, slot, to):
+        return pltpu.make_async_remote_copy(
+            src_ref=kvbuf.at[block], dst_ref=kvbuf.at[block], send_sem=kv_send.at[slot],
+            recv_sem=kv_recv.at[block], device_id=(to, e), device_id_type=MESH,
+        )
+
+    def w_copy(block, g, sem, to):
+        return pltpu.make_async_remote_copy(
+            src_ref=wbuf.at[block, g], dst_ref=wbuf.at[block, g], send_sem=sem,
+            recv_sem=w_recv.at[block, g], device_id=(to, e), device_id_type=MESH,
+        )
+
+    for step in range(1, N_Z):
+        kv_copy(c, step - 1, ((z + step) % N_Z) * PLANE + plane).start()
+    kv_copy(c, 3, y_peer).start()
+    kv_copy(c, 7, sibling).start()
+    swap = pltpu.make_async_remote_copy(
+        src_ref=w_hbm.at[:, pl.ds(pl.multiple_of((1 - e) * half, half), half)],
+        dst_ref=wbuf.at[c, e], send_sem=x_send.at[0], recv_sem=w_recv.at[c, e],
+        device_id=(c, 1 - e), device_id_type=MESH,
+    )
+    swap.start()
+
+    def group_of(s):
+        return (e + s) % 2
+
+    def z_forward(block_z, s, up, down):
+        g = group_of(s)
+        block = block_z * PLANE + plane
+
+        @pl.when(jnp.logical_and(up, z < N_Z - 1))
+        def _():
+            w_copy(block, g, w_up.at[block_z, g], c + PLANE).start()
+
+        @pl.when(jnp.logical_and(down, z > 0))
+        def _():
+            w_copy(block, g, w_down_sem.at[block_z, g], c - PLANE).start()
+
+        w_copy(block, g, w_y.at[block_z, g], y_peer).start()
+        w_copy(block, g, w_sib.at[0, block_z, g], sibling).start()
+
+    def wait_block(block, g):
+        w_copy(block, g, w_sib.at[0, 0, 0], sibling).wait_recv()
+
+    own_w.wait()
+    z_forward(z, 0, True, True)
+
+    for step in range(1, N_Z):
+        block = ((z + step) % N_Z) * PLANE + plane
+        kv_copy(block, 0, sibling).wait_recv()
+        kv_copy(block, 3 + step, y_peer).start()
+        kv_copy(block, 7 + step, sibling).start()
+    for step in range(N_Z):
+        block = ((z + step) % N_Z) * PLANE + (1 - y) * 2 + k
+        kv_copy(block, 0, sibling).wait_recv()
+        kv_copy(block, 11 + step, sibling).start()
+    rows32[...] = q_ref[...].astype(F32)
+    row = lax.broadcasted_iota(jnp.int32, target.shape, 0)
+    col = lax.broadcasted_iota(jnp.int32, target.shape, 1)
+    target[...] = row - ((col % 128) // 8) * 128 - (col // 128) * 8 - col % 8
+    wait_block(c, group_of(1))
+    z_forward(z, 1, True, True)
+    for block_z in range(N_Z):
+        for block_y in range(2):
+            kv_copy(block_z * PLANE + block_y * 2 + 1 - k, 0, sibling).wait_recv()
+
+    scale = 1.0 / math.sqrt(q_ref.shape[1])
+    n_keys = kvbuf.shape[0] * tokens
+
+    @pl.loop(0, heads // 2)
+    def _(pair):
+        first = rows32[pl.ds(2 * pair, tokens, stride=heads), :]
+        second = rows32[pl.ds(2 * pair + 1, tokens, stride=heads), :]
+        both = jnp.concatenate([first, second], axis=0).astype(BF16)
+        key_all = kvbuf[:, :tokens, :].reshape(n_keys, 128)
+        value_all = kvbuf[:, tokens:, :].reshape(n_keys, 128)
+        scores = lax.dot_general(
+            both, key_all, (((1,), (1,)), ((), ())), preferred_element_type=F32
+        ) * scale
+        q_pos = c * tokens + lax.broadcasted_iota(jnp.int32, scores.shape, 0) % tokens
+        k_pos = lax.broadcasted_iota(jnp.int32, scores.shape, 1)
+        masked = jnp.where(k_pos <= q_pos, scores, masked_score)
+        best = jnp.max(masked, axis=1, keepdims=True)
+        prob = jnp.exp(masked - best)
+        total = jnp.sum(prob, axis=1, keepdims=True)
+        part = jnp.dot(prob.astype(BF16), value_all, preferred_element_type=F32)
+        done = (part / total).astype(BF16)
+        ctx2d[:, pl.ds(pl.multiple_of(pair * 256, 256), 128)] = done[:tokens]
+        ctx2d[:, pl.ds(pl.multiple_of(pair * 256 + 128, 128), 128)] = done[tokens:]
+        rows32[pl.ds(2 * pair, tokens, stride=heads), :] = done[:tokens].astype(F32)
+        rows32[pl.ds(2 * pair + 1, tokens, stride=heads), :] = done[tokens:].astype(F32)
+
+    @pl.loop(0, wbuf.shape[0] // 2)
+    def _(pair):
+        pick = jnp.where(target[...] == 16 * pair, 1.0, 0.0).astype(BF16)
+        ctxbuf[e, pair] = jnp.dot(ctx2d[...], pick, preferred_element_type=F32).astype(BF16)
+
+    ctx_swap = pltpu.make_async_remote_copy(
+        src_ref=ctxbuf.at[e], dst_ref=ctxbuf.at[e], send_sem=c_send.at[0], recv_sem=c_recv.at[0],
+        device_id=(c, 1 - e), device_id_type=MESH,
+    )
+    ctx_swap.start()
+    ctx_ref[...] = rows32[...].astype(BF16)
+    acc[...] = jnp.zeros_like(acc)
+    other_ctx = pltpu.make_async_remote_copy(
+        src_ref=ctxbuf.at[1 - e], dst_ref=ctxbuf.at[1 - e], send_sem=c_send.at[0],
+        recv_sem=c_recv.at[0], device_id=(c, 1 - e), device_id_type=MESH,
+    )
+
+    def sides(i, run):
+        d = i // 2
+
+        @pl.when(z - d >= 0)
+        def _():
+            run(z - d, True, False)
+
+        @pl.when(jnp.logical_and(d > 0, z + d < N_Z))
+        def _():
+            run(z + d, False, True)
+
+    def project(block_z, block_y, g):
+        pair = block_z * 2 + block_y
+        weights = wbuf[pl.ds(2 * pair, 2), pl.ds(g, 1)].reshape(2 * depth, half)
+        acc[g] += jnp.dot(ctxbuf[g, pair], weights, preferred_element_type=F32)
+
+    @pl.loop(0, 2 * N_Z)
+    def _(i):
+        s = i % 2
+        g = group_of(s)
+
+        @pl.when(i + 2 < 2 * N_Z)
+        def _():
+            def run(block_z, up, down):
+                wait_block(block_z * PLANE + plane, g)
+                z_forward(block_z, s, up, down)
+
+            sides(i + 2, run)
+
+        def run_y(block_z, up, down):
+            block = block_z * PLANE + (1 - y) * 2 + k
+            wait_block(block, g)
+            w_copy(block, g, w_sib.at[1, block_z, g], sibling).start()
+
+        sides(i, run_y)
+
+        @pl.when(i == 1)
+        def _():
+            other_ctx.wait_recv()
+
+        def run_project(block_z, up, down):
+            wait_block(block_z * PLANE + y * 2 + 1 - k, g)
+            project(block_z, y, g)
+            wait_block(block_z * PLANE + (1 - y) * 2 + 1 - k, g)
+            project(block_z, 1 - y, g)
+
+        sides(i, run_project)
+
+    hid_ref[...] = resid_ref[...].astype(F32) + (
+        acc[0].astype(BF16).astype(F32) + acc[1].astype(BF16).astype(F32)
+    )
+
+    for slot in range(15):
+        kv_copy(c, slot, sibling).wait_send()
+    swap.wait_send()
+    ctx_swap.wait_send()
+
+    @pl.loop(0, N_Z)
+    def _(block_z):
+        for g in range(2):
+            @pl.when(jnp.logical_and(block_z <= z, z < N_Z - 1))
+            def _():
+                w_copy(c, g, w_up.at[block_z, g], sibling).wait_send()
+
+            @pl.when(jnp.logical_and(block_z >= z, z > 0))
+            def _():
+                w_copy(c, g, w_down_sem.at[block_z, g], sibling).wait_send()
+
+            w_copy(c, g, w_y.at[block_z, g], sibling).wait_send()
+            w_copy(c, g, w_sib.at[0, block_z, g], sibling).wait_send()
+            w_copy(c, g, w_sib.at[1, block_z, g], sibling).wait_send()
+
+
+def expert_kernel(
+    hid_ref, gain_ref, pick_ref, mix_ref, gu_hbm, down_hbm, mixed_ref,
+    gu, down, squares, peer_squares, stage, two, outbox, inbox, backbox, endbox, parts, peer_parts, act,
+    sq_sem, p_send, p_recv, a_send, a_recv, b_send, b_recv, local_sem,
+):
+    c = lax.axis_index("ctx")
+    e = lax.axis_index("exp")
+    n = inbox.shape[0]
+    cap = inbox.shape[1]
+    rows = n * cap
+    blocks = inbox.shape[2]
+    barrier = pltpu.get_barrier_semaphore()
+
+    @pl.loop(1, n)
+    def _(j):
+        pl.semaphore_signal(barrier, inc=1, device_id=((c + j) % n, e), device_id_type=MESH)
+
+    pl.semaphore_signal(barrier, inc=1, device_id=(c, 1 - e), device_id_type=MESH)
+    load_gu = pltpu.make_async_copy(gu_hbm, gu, local_sem.at[0])
+    load_down = pltpu.make_async_copy(down_hbm, down, local_sem.at[1])
+    load_gu.start()
+    load_down.start()
+    hidden = hid_ref[...]
+    own = jnp.sum(hidden * hidden, axis=1, keepdims=True)
+    squares[...] = jnp.broadcast_to(own, squares.shape)
+    pl.semaphore_wait(barrier, n)
+    sq = pltpu.make_async_remote_copy(
+        src_ref=squares, dst_ref=peer_squares, send_sem=sq_sem.at[0], recv_sem=sq_sem.at[1],
+        device_id=(c, 1 - e), device_id_type=MESH,
+    )
+    sq.start()
+    sq.wait()
+    mean = (squares[:, :1] + peer_squares[:, :1]) / D
+    normed = (hid_ref[...] * lax.rsqrt(mean + epsilon) * gain_ref[...]).astype(BF16)
+    two[: normed.shape[0], :] = normed
+    for j in range(blocks):
+        stage[pl.ds(j, rows, stride=blocks), :] = jnp.dot(
+            pick_ref[...], two[: normed.shape[0], j * 128 : (j + 1) * 128], preferred_element_type=F32
+        )
+    outbox[...] = stage[...].reshape(outbox.shape).astype(BF16)
+
+    def a_copy(j):
+        to = (c + j) % n
+        return pltpu.make_async_remote_copy(
+            src_ref=outbox.at[to], dst_ref=inbox.at[c], send_sem=a_send.at[j],
+            recv_sem=a_recv.at[c], device_id=(to, e), device_id_type=MESH,
+        )
+
+    def b_copy(j):
+        to = (c + j) % n
+        return pltpu.make_async_remote_copy(
+            src_ref=backbox.at[to], dst_ref=endbox.at[c], send_sem=b_send.at[j],
+            recv_sem=b_recv.at[c], device_id=(to, e), device_id_type=MESH,
+        )
+
+    def arrived(box, sems):
+        @pl.loop(1, n)
+        def _(j):
+            source = (c + j) % n
+            pltpu.make_async_remote_copy(
+                src_ref=box.at[source], dst_ref=box.at[source], send_sem=a_send.at[0],
+                recv_sem=sems.at[source], device_id=(source, e), device_id_type=MESH,
+            ).wait_recv()
+
+        stage[...] = box[...].reshape(stage.shape).astype(F32)
+        for j in range(blocks):
+            two[:, j * 128 : (j + 1) * 128] = stage[pl.ds(j, rows, stride=blocks), :].astype(BF16)
+
+    @pl.loop(1, n)
+    def _(j):
+        a_copy(j).start()
+
+    inbox[c] = outbox[c]
+    load_gu.wait()
+    arrived(inbox, a_recv)
+
+    units = down.shape[0]
+    width = parts.shape[3]
+
+    def p_copy(m):
+        return pltpu.make_async_remote_copy(
+            src_ref=parts.at[m], dst_ref=peer_parts.at[m], send_sem=p_send.at[m],
+            recv_sem=p_recv.at[m], device_id=(c, 1 - e), device_id_type=MESH,
+        )
+
+    n_parts = units // width
+    for m in range(n_parts):
+        for side in range(2):
+            start = side * units + m * width
+            parts[m, side] = jnp.dot(
+                two[...], gu[:, start : start + width], preferred_element_type=F32
+            ).astype(BF16)
+        p_copy(m).start()
+    for m in range(n_parts):
+        p_copy(m).wait_recv()
+        gate = parts[m, 0].astype(F32) + peer_parts[m, 0].astype(F32)
+        up = parts[m, 1].astype(F32) + peer_parts[m, 1].astype(F32)
+        act[:, m * width : (m + 1) * width] = (gate / (1.0 + jnp.exp(-gate)) * up).astype(BF16)
+    load_down.wait()
+    for j in range(blocks // 2):
+        result = jnp.dot(
+            act[...], down[:, j * 256 : (j + 1) * 256], preferred_element_type=F32
+        )
+        stage[pl.ds(2 * j, rows, stride=blocks), :] = result[:, :128]
+        stage[pl.ds(2 * j + 1, rows, stride=blocks), :] = result[:, 128:]
+    backbox[...] = stage[...].reshape(backbox.shape).astype(BF16)
+
+    @pl.loop(1, n)
+    def _(j):
+        b_copy(j).start()
+
+    endbox[c] = backbox[c]
+    mix = mix_ref[...]
+    mix_high = mix.astype(BF16)
+    mix_low = (mix - mix_high.astype(F32)).astype(BF16)
+    arrived(endbox, b_recv)
+    routed = jnp.dot(mix_high, two[...], preferred_element_type=F32)
+    routed += jnp.dot(mix_low, two[...], preferred_element_type=F32)
+    mixed_ref[...] = (hid_ref[...] + routed).astype(BF16)
+
+    @pl.loop(1, n)
+    def _(j):
+        a_copy(j).wait_send()
+        b_copy(j).wait_send()
+
+    for m in range(n_parts):
+        p_copy(m).wait_send()
+
+
+def fast_body(queries, keys, values, resid, gain, expert_ids, gate_scores, w_gate_up, w_down, w_out):
+    tokens, heads, size = queries.shape
+    n = lax.axis_size("ctx")
+    exp_place = lax.axis_index("exp")
+    half = resid.shape[1]
+    capacity = max(2, 5 * tokens * TOPK // (4 * EXPERTS))
+    hits = expert_ids[:, :, None] == jnp.arange(n, dtype=jnp.int32)[None, None, :]
+    named = jnp.any(hits, axis=1)
+    earlier = jnp.tril(jnp.ones((tokens, tokens), BF16), -1)
+    rank = jnp.dot(earlier, named.astype(BF16), preferred_element_type=F32).astype(jnp.int32)
+    rank = jnp.where(named, rank, -1)
+    slots = jnp.arange(capacity, dtype=jnp.int32)
+    pick = (rank.T[:, None, :] == slots[None, :, None]).astype(BF16).reshape(n * capacity, tokens)
+    share = gate_scores / jnp.sum(gate_scores, axis=1, keepdims=True)
+    share = jnp.sum(jnp.where(hits, share[:, :, None], 0.0), axis=1)
+    mix = jnp.where(rank[:, :, None] == slots[None, None, :], share[:, :, None], 0.0)
+    mix = mix.reshape(tokens, n * capacity)
+
+    group = exp_place * heads // (HQ // KVH)
+    own_kv = jnp.concatenate(
+        [
+            lax.dynamic_index_in_dim(keys, group, 1, keepdims=False),
+            lax.dynamic_index_in_dim(values, group, 1, keepdims=False),
+        ],
+        axis=0,
+    )
+    depth = heads * w_out.shape[1]
+    vmem = pl.BlockSpec(memory_space=pltpu.VMEM)
+    hbm = pl.BlockSpec(memory_space=pl.ANY)
+    dma = pltpu.SemaphoreType.DMA
+    context, hidden = pl.pallas_call(
+        attend_kernel,
+        out_shape=(
+            jax.ShapeDtypeStruct((tokens * heads, size), BF16),
+            jax.ShapeDtypeStruct((tokens, half), F32),
+        ),
+        in_specs=[vmem, vmem, hbm, vmem],
+        out_specs=(vmem, vmem),
+        scratch_shapes=[
+            pltpu.VMEM((n, 2 * tokens, size), BF16),
+            pltpu.VMEM((n, 2, depth, half), BF16),
+            pltpu.VMEM((tokens * heads, size), F32),
+            pltpu.VMEM((tokens, heads * size), BF16),
+            pltpu.VMEM((2, n // 2, tokens, 2 * depth), BF16),
+            pltpu.VMEM((heads * size, 2 * depth), jnp.int32),
+            pltpu.VMEM((2, tokens, half), F32),
+            dma((15,)), dma((n,)), dma((N_Z, 2)), dma((N_Z, 2)), dma((N_Z, 2)),
+            dma((2, N_Z, 2)), dma((n, 2)), dma((1,)), dma((1,)), dma((1,)), dma((1,)),
+        ],
+        compiler_params=pltpu.CompilerParams(
+            collective_id=0, has_side_effects=True, vmem_limit_bytes=50 * 2**20
+        ),
+        name="attend",
+    )(queries.reshape(tokens * heads, size), own_kv, w_out.reshape(depth, 2 * half), resid)
+
+    units = w_down.shape[1]
+    rows = n * capacity
+    blocks = half // 128
+    box = (n, capacity, blocks, 128)
+    width = 256
+    mixed = pl.pallas_call(
+        expert_kernel,
+        out_shape=jax.ShapeDtypeStruct((tokens, half), BF16),
+        in_specs=[vmem, vmem, vmem, vmem, hbm, hbm],
+        out_specs=vmem,
+        scratch_shapes=[
+            pltpu.VMEM((half, 2 * units), BF16),
+            pltpu.VMEM((units, half), BF16),
+            pltpu.VMEM((tokens, 128), F32),
+            pltpu.VMEM((tokens, 128), F32),
+            pltpu.VMEM((rows * blocks, 128), F32),
+            pltpu.VMEM((rows, half), BF16),
+            pltpu.VMEM(box, BF16), pltpu.VMEM(box, BF16), pltpu.VMEM(box, BF16), pltpu.VMEM(box, BF16),
+            pltpu.VMEM((units // width, 2, rows, width), BF16),
+            pltpu.VMEM((units // width, 2, rows, width), BF16),
+            pltpu.VMEM((rows, units), BF16),
+            dma((2,)), dma((units // width,)), dma((units // width,)),
+            dma((n,)), dma((n,)), dma((n,)), dma((n,)), dma((2,)),
+        ],
+        compiler_params=pltpu.CompilerParams(
+            collective_id=1, has_side_effects=True, vmem_limit_bytes=50 * 2**20
+        ),
+        name="experts",
+    )(
+        hidden, gain.reshape(1, half), pick, mix,
+        w_gate_up[0].reshape(half, 2 * units), w_down[0],
+    )
+    return (context.reshape(tokens, heads, size), mixed)
+
+
 def solution(mesh):
     in_specs = (
         P("ctx", "exp", None),
@@ -157,4 +601,6 @@
         P("exp", "ctx", None),
     )
     out_specs = (P("ctx", "exp", None), P("ctx", "exp"))
+    fits = mesh.shape["ctx"] == N_Z * PLANE and mesh.shape["exp"] == 2
+    body = fast_body if fits else general_body
     return jax.shard_map(body, mesh=mesh, in_specs=in_specs, out_specs=out_specs, check_vma=False)

time: 314 us -> 178 us (0.57)
  the two profiles are of different devices: /device:TPU:1 before, /device:TPU:25 now
where the time goes in v1:
time: 178 us; the launch traced here: 177 us
  Pallas kernels  160 us (90%)
  local copies, waits for them, and re-layouts  13.1 us (7%)
  other arithmetic  2.92 us (2%)
    pallas_call x1, Pallas kernels, fast_body(): pl.pallas_call(attend_kernel, out_shape=(jax.ShapeDtypeStruct((tokens * h...  106 us
    pallas_call x1, Pallas kernels, fast_body(): pl.pallas_call(expert_kernel, out_shape=jax.ShapeDtypeStruct((tokens, hal...  54.2 us
    unnamed x13, local copies, waits for them, and re-layouts  11.7 us

profile of v1, /device:TPU:25, one launch (start us, length us, event | category | flops | bytes accessed | tf_op | source)
XLA Modules:
  0.0 177.5 jit_solution(17257236313512768438)
XLA Ops:
  0.6 0.7 reduce_sum.18
  1.4 0.7 fusion.1
  2.1 0.7 broadcast_divide_fusion
  2.8 0.7 select_reduce_fusion
  3.5 0.2 fusion
  3.7 0.1 eq.59
  3.8 0.1 copy.24
  3.9 1.0 constant_dynamic-slice_fusion
  5.0 0.1 compare_convert_fusion.pick_ref
  5.1 0.1 copy.23
  5.3 0.0 copy-start
  5.3 1.2 copy-done
  6.5 0.0 copy-start.1
  6.5 1.0 copy-done.1
  7.5 0.0 copy-start.2
  7.5 1.0 copy-done.2
  8.6 106.3 %attend.1 = (bf16[2048,128]{1,0:T(8,128)(2,1)S(1)}, f32[128,2048]{1,0:T(8,128)S(1)}) custom-call(bf16[2048,128]{1,0:T(8,128)(2,1)S(1)} %bitcast.22, bf16[256,128]{1,0:T(8,128)(2,1)S(1)} %pad_maximum_fusion.kv_ref, bf16[128,4096]{1,0:T(8,128)(2,1)S(1)} %bitcast.20, bf16[128,2048]{1,0:T(8,128)(2,1)S(1)} %copy-done.2), custom_call_target="tpu_custom_call" | custom-call | tf_op jit(solution)/shard_map/attend/pallas_call | solution.py:530
  114.9 0.0 copy-start.3
  114.9 6.8 %copy.27 = bf16[256,8,2,768]{3,1,2,0:T(8,128)(2,1)} copy(bf16[256,8,2,768]{3,2,1,0:T(2,128)(2,1)} %bitcast.25) | data formatting | bytes 12582912
  121.7 0.0 copy-done.3
  121.7 54.2 %experts.1 = bf16[128,2048]{1,0:T(8,128)(2,1)S(1)} custom-call(f32[128,2048]{1,0:T(8,128)S(1)} %get-tuple-element.5.hid_ref, f32[1,2048]{1,0:T(1,128)S(1)} %bitcast.23, bf16[160,128]{1,0:T(8,128)(2,1)S(1)} %compare_convert_fusion.pick_ref, f32[128,160]{1,0:T(8,128)S(1)} %compare_select_fusion.mix_ref, bf16[2048,1536]{1,0:T(8,128)(2,1)} %bitcast.24, ...), custom_call_target="tpu_custom_call" | custom-call | tf_op jit(solution)/shard_map/experts/pallas_call | solution.py:560
  175.9 0.8 copy.34
  176.7 0.8 copy.35
  (12 shorter events, 0.1 us)
Async XLA Ops:
  5.3 1.2 copy-start
  6.5 1.0 copy-start.1
  7.5 1.0 copy-start.2
  114.9 6.8 %copy-start.3 = (f32[2048]{0:T(1024)S(1)}, f32[2048]{0:T(1024)}, u32[]{:S(2)}) copy-start(f32[2048]{0:T(1024)} %param.14) | copy-start | bytes 24580

commit v2 on v0

--- a/solution.py
+++ b/solution.py
@@ -1,8 +1,11 @@
+import functools
 import math
 
 import jax
 import jax.numpy as jnp
 from jax import lax
+from jax.experimental import pallas as pl
+from jax.experimental.pallas import tpu as pltpu
 from jax.sharding import PartitionSpec as P
 
 D = 4096
@@ -42,7 +45,7 @@
     return lax.cond(offset <= last_pos, compute, untouched, state_now)
 
 
-def body(queries, keys, values, resid, gain, expert_ids, gate_scores, w_gate_up, w_down, w_out):
+def general_body(queries, keys, values, resid, gain, expert_ids, gate_scores, w_gate_up, w_down, w_out):
     tokens_here = queries.shape[0]
     heads_here = queries.shape[1]
     head_size = queries.shape[2]
@@ -143,6 +146,503 @@
     return (context, mixed)
 
 
+MESH = pl.DeviceIdType.MESH
+F32 = jnp.float32
+BF16 = jnp.bfloat16
+N_Z = 4
+PLANE = 4
+HALF_Z = 8
+
+
+def layer_kernel(
+    q_hbm, key_ref, value_ref, w_hbm, resid_hbm, gain_ref, ids_ref, gate_ref, gu_hbm, down_hbm,
+    ctx_ref, mixed_ref,
+    q_in, resid, kvbuf, wbuf, rows32, ctx2d, ctxbuf, target, acc, part_out, part_in,
+    gu_raw, gu, down, squares, peer_squares, hidden_buf, stage, two, outbox, inbox, backbox, endbox,
+    parts, peer_parts, act,
+    kv_send, kv_recv, own_z, fwd_z, own_y, fwd_y, w_sib, w_recv, x_send, c_send, c_recv, h_send, h_recv,
+    sq_sem, p_send, p_recv, a_send, a_recv, b_send, b_recv, local_sem,
+):
+    c = lax.axis_index("ctx")
+    e = lax.axis_index("exp")
+    n = inbox.shape[0]
+    cap = inbox.shape[1]
+    rows = n * cap
+    blocks = inbox.shape[2]
+    z = c // PLANE
+    zh = z // 2
+    zl = z % 2
+    y = (c // 2) % 2
+    k = c % 2
+    plane = c % PLANE
+    z_peer = c + PLANE * (1 - 2 * zl)
+    y_peer = c + 2 * (1 - 2 * y)
+    sibling = c + 1 - 2 * k
+    partner = c + HALF_Z * (1 - 2 * zh)
+    half = resid.shape[1]
+    tokens = resid.shape[0]
+    heads = q_in.shape[0] // tokens
+    wide = wbuf.shape[4]
+    depth = wbuf.shape[3]
+
+    def block_of(other_z, other_y, other_k):
+        in_z = zl + other_z * (1 - 2 * zl)
+        in_y = y + other_y * (1 - 2 * y)
+        in_k = k + other_k * (1 - 2 * k)
+        return in_z * PLANE + in_y * 2 + in_k
+
+    barrier = pltpu.get_barrier_semaphore()
+
+    @pl.loop(1, n)
+    def _(j):
+        pl.semaphore_signal(barrier, inc=1, device_id=((c + j) % n, e), device_id_type=MESH)
+
+    pl.semaphore_signal(barrier, inc=1, device_id=(c, 1 - e), device_id_type=MESH)
+    mine = block_of(0, 0, 0)
+
+    def own_load(f):
+        return pltpu.make_async_copy(
+            w_hbm.at[:, pl.ds(pl.multiple_of(e * half + f * wide, wide), wide)],
+            wbuf.at[f, mine, e], local_sem.at[f],
+        )
+
+    load_q = pltpu.make_async_copy(q_hbm, q_in, local_sem.at[2])
+    load_resid = pltpu.make_async_copy(resid_hbm, resid, local_sem.at[3])
+    load_gu = pltpu.make_async_copy(gu_hbm, gu_raw, local_sem.at[4])
+    load_down = pltpu.make_async_copy(down_hbm, down, local_sem.at[5])
+    own_load(0).start()
+    own_load(1).start()
+    load_q.start()
+    load_resid.start()
+    load_gu.start()
+    load_down.start()
+    lane = pl.ds(pl.multiple_of(e * 128, 128), 128)
+    kvbuf[c, :tokens, :] = key_ref[:, lane]
+    kvbuf[c, tokens:, :] = value_ref[:, lane]
+    pl.semaphore_wait(barrier, n)
+
+    def kv_copy(block, slot, to):
+        return pltpu.make_async_remote_copy(
+            src_ref=kvbuf.at[block], dst_ref=kvbuf.at[block], send_sem=kv_send.at[slot],
+            recv_sem=kv_recv.at[block], device_id=(to, e), device_id_type=MESH,
+        )
+
+    def w_copy(block, f, g, sem, to):
+        return pltpu.make_async_remote_copy(
+            src_ref=wbuf.at[f, block, g], dst_ref=wbuf.at[f, block, g], send_sem=sem,
+            recv_sem=w_recv.at[block, f, g], device_id=(to, e), device_id_type=MESH,
+        )
+
+    def wait_block(block, f, g):
+        w_copy(block, f, g, own_z.at[0, 0], sibling).wait_recv()
+
+    def swap(f):
+        return pltpu.make_async_remote_copy(
+            src_ref=w_hbm.at[:, pl.ds(pl.multiple_of((1 - e) * half + f * wide, wide), wide)],
+            dst_ref=wbuf.at[f, mine, e], send_sem=x_send.at[f], recv_sem=w_recv.at[mine, f, e],
+            device_id=(c, 1 - e), device_id_type=MESH,
+        )
+
+    def group_of(s):
+        return (e + s) % 2
+
+    def send_own(f, s):
+        g = group_of(s)
+        w_copy(mine, f, g, own_z.at[f, g], z_peer).start()
+        w_copy(mine, f, g, own_y.at[f, g], y_peer).start()
+        w_copy(mine, f, g, w_sib.at[0, f, g], sibling).start()
+
+    for step in range(1, N_Z):
+        kv_copy(c, step - 1, ((z + step) % N_Z) * PLANE + plane).start()
+    kv_copy(c, 3, y_peer).start()
+    kv_copy(c, 7, sibling).start()
+    swap(0).start()
+    swap(1).start()
+    own_load(0).wait()
+    send_own(0, 0)
+    load_q.wait()
+    rows32[...] = q_in[...].astype(F32)
+    for step in range(1, N_Z):
+        block = ((z + step) % N_Z) * PLANE + plane
+        kv_copy(block, 0, sibling).wait_recv()
+        kv_copy(block, 3 + step, y_peer).start()
+        kv_copy(block, 7 + step, sibling).start()
+    wait_block(mine, 0, group_of(1))
+    send_own(0, 1)
+    own_load(1).wait()
+    send_own(1, 0)
+    wait_block(mine, 1, group_of(1))
+    send_own(1, 1)
+    for step in range(N_Z):
+        block = ((z + step) % N_Z) * PLANE + (1 - y) * 2 + k
+        kv_copy(block, 0, sibling).wait_recv()
+        kv_copy(block, 11 + step, sibling).start()
+    row = lax.broadcasted_iota(jnp.int32, target.shape, 0)
+    col = lax.broadcasted_iota(jnp.int32, target.shape, 1)
+    target[...] = row - ((col % 128) // 8) * 128 - (col // 128) * 8 - col % 8
+    for block_z in range(N_Z):
+        for block_y in range(2):
+            kv_copy(block_z * PLANE + block_y * 2 + 1 - k, 0, sibling).wait_recv()
+
+    scale = 1.0 / math.sqrt(q_in.shape[1])
+    n_keys = n * tokens
+
+    def attend(pair):
+        first = rows32[pl.ds(2 * pair, tokens, stride=heads), :]
+        second = rows32[pl.ds(2 * pair + 1, tokens, stride=heads), :]
+        both = jnp.concatenate([first, second], axis=0).astype(BF16)
+        key_all = kvbuf[:, :tokens, :].reshape(n_keys, 128)
+        value_all = kvbuf[:, tokens:, :].reshape(n_keys, 128)
+        scores = lax.dot_general(
+            both, key_all, (((1,), (1,)), ((), ())), preferred_element_type=F32
+        ) * scale
+        q_pos = c * tokens + lax.broadcasted_iota(jnp.int32, scores.shape, 0) % tokens
+        k_pos = lax.broadcasted_iota(jnp.int32, scores.shape, 1)
+        masked = jnp.where(k_pos <= q_pos, scores, masked_score)
+        best = jnp.max(masked, axis=1, keepdims=True)
+        prob = jnp.exp(masked - best)
+        total = jnp.sum(prob, axis=1, keepdims=True)
+        part = jnp.dot(prob.astype(BF16), value_all, preferred_element_type=F32)
+        done = (part / total).astype(BF16)
+        ctx2d[:, pl.ds(pl.multiple_of(pair * 256, 256), 128)] = done[:tokens]
+        ctx2d[:, pl.ds(pl.multiple_of(pair * 256 + 128, 128), 128)] = done[tokens:]
+        rows32[pl.ds(2 * pair, tokens, stride=heads), :] = done[:tokens].astype(F32)
+        rows32[pl.ds(2 * pair + 1, tokens, stride=heads), :] = done[tokens:].astype(F32)
+
+    @pl.loop(0, 2)
+    def _(turn):
+        @pl.loop(0, heads // 4)
+        def _(step):
+            attend(turn * (heads // 4) + step)
+
+        @pl.when(turn == 0)
+        def _():
+            @pl.loop(0, 2)
+            def _(s):
+                g = group_of(s)
+                wait_block(block_of(1, 0, 0), 0, g)
+                w_copy(block_of(1, 0, 0), 0, g, fwd_y.at[g], y_peer).start()
+                w_copy(block_of(1, 0, 0), 0, g, w_sib.at[1, 0, g], sibling).start()
+                wait_block(block_of(0, 1, 0), 0, g)
+                w_copy(block_of(0, 1, 0), 0, g, w_sib.at[2, 0, g], sibling).start()
+
+    def pick_pair(pair):
+        pick = jnp.where(target[...] == 16 * pair, 1.0, 0.0).astype(BF16)
+        return jnp.dot(ctx2d[...], pick, preferred_element_type=F32).astype(BF16)
+
+    n_pairs = ctxbuf.shape[2]
+
+    @pl.loop(0, n_pairs)
+    def _(pair):
+        ctxbuf[2, 0, pair] = pick_pair((1 - zh) * n_pairs + pair)
+
+    def ctx_copy(slot, src, dst, to):
+        return pltpu.make_async_remote_copy(
+            src_ref=src, dst_ref=dst, send_sem=c_send.at[slot], recv_sem=c_recv.at[slot],
+            device_id=to, device_id_type=MESH,
+        )
+
+    to_partner = ctx_copy(0, ctxbuf.at[2, 0], ctxbuf.at[1, e], (partner, e))
+    to_partner.start()
+
+    @pl.loop(0, n_pairs)
+    def _(pair):
+        ctxbuf[0, e, pair] = pick_pair(zh * n_pairs + pair)
+
+    own_over = ctx_copy(1, ctxbuf.at[0, e], ctxbuf.at[0, e], (c, 1 - e))
+    own_over.start()
+
+    @pl.loop(0, 2)
+    def _(s):
+        g = group_of(s)
+        wait_block(block_of(0, 1, 0), 1, g)
+        w_copy(block_of(0, 1, 0), 1, g, fwd_z.at[g], z_peer).start()
+        w_copy(block_of(0, 1, 0), 1, g, w_sib.at[2, 1, g], sibling).start()
+        wait_block(block_of(1, 0, 0), 1, g)
+        w_copy(block_of(1, 0, 0), 1, g, w_sib.at[1, 1, g], sibling).start()
+
+    units = down.shape[0]
+    unpack_rows = 128
+
+    def unpack(first, count):
+        @pl.loop(first, first + count)
+        def _(i):
+            at = pl.ds(pl.multiple_of(i * unpack_rows, unpack_rows), unpack_rows)
+            gu[at, :units] = gu_raw[at, 0, :]
+            gu[at, units:] = gu_raw[at, 1, :]
+
+    n_unpack = half // unpack_rows
+    load_gu.wait()
+    unpack(0, n_unpack // 4)
+    pltpu.make_async_remote_copy(
+        src_ref=ctxbuf.at[1, e], dst_ref=ctxbuf.at[1, e], send_sem=c_send.at[0],
+        recv_sem=c_recv.at[0], device_id=(partner, e), device_id_type=MESH,
+    ).wait_recv()
+    partner_over = ctx_copy(2, ctxbuf.at[1, e], ctxbuf.at[1, e], (c, 1 - e))
+    partner_over.start()
+
+    def relay_far(f):
+        @pl.loop(0, 2)
+        def _(s):
+            g = group_of(s)
+            wait_block(block_of(1, 1, 0), f, g)
+            w_copy(block_of(1, 1, 0), f, g, w_sib.at[3, f, g], sibling).start()
+
+    relay_far(0)
+    unpack(n_unpack // 4, n_unpack // 4)
+    ctx_ref[...] = rows32[...].astype(BF16)
+    acc[...] = jnp.zeros_like(acc)
+    for slot in range(2):
+        pltpu.make_async_remote_copy(
+            src_ref=ctxbuf.at[slot, 1 - e], dst_ref=ctxbuf.at[slot, 1 - e], send_sem=c_send.at[0],
+            recv_sem=c_recv.at[1 + slot], device_id=(c, 1 - e), device_id_type=MESH,
+        ).wait_recv()
+
+    def project(f):
+        @pl.loop(0, 8)
+        def _(i):
+            other_z = i // 4
+            other_y = (i // 2) % 2
+            g = group_of(i % 2)
+            wait_block(block_of(other_z, other_y, 1), f, g)
+            first = block_of(other_z, other_y, 0)
+            pair = first // 2
+            weights = wbuf[f, pl.ds(2 * pair, 2), pl.ds(g, 1)].reshape(2 * depth, wide)
+            lhs = jnp.concatenate([ctxbuf[0, g, pair], ctxbuf[1, g, pair]], axis=0)
+            acc[f] += jnp.dot(lhs, weights, preferred_element_type=F32)
+
+        part_out[f] = acc[f, tokens:, :].astype(BF16)
+        pltpu.make_async_remote_copy(
+            src_ref=part_out.at[f], dst_ref=part_in.at[f], send_sem=h_send.at[f],
+            recv_sem=h_recv.at[f], device_id=(partner, e), device_id_type=MESH,
+        ).start()
+
+    def part_copy(f):
+        return pltpu.make_async_remote_copy(
+            src_ref=part_out.at[f], dst_ref=part_in.at[f], send_sem=h_send.at[f],
+            recv_sem=h_recv.at[f], device_id=(partner, e), device_id_type=MESH,
+        )
+
+    project(0)
+    relay_far(1)
+    project(1)
+    load_resid.wait()
+    unpack(n_unpack // 2, n_unpack // 4)
+
+    slot = lax.broadcasted_iota(jnp.int32, (tokens, rows), 1)
+    named = jnp.zeros((tokens, rows), F32)
+    share = jnp.zeros((tokens, rows), F32)
+    gates = gate_ref[...]
+    gates = gates / jnp.sum(gates, axis=1, keepdims=True)
+    for column in range(TOPK):
+        hit = ids_ref[:, column : column + 1] == slot // cap
+        named = jnp.where(hit, 1.0, named)
+        share = jnp.where(hit, gates[:, column : column + 1], share)
+    before = jnp.where(
+        lax.broadcasted_iota(jnp.int32, (tokens, tokens), 1)
+        < lax.broadcasted_iota(jnp.int32, (tokens, tokens), 0),
+        1.0,
+        0.0,
+    ).astype(BF16)
+    rank = jnp.dot(before, named.astype(BF16), preferred_element_type=F32)
+    chosen = jnp.logical_and(named > 0.5, rank == (slot % cap).astype(F32))
+    pick = jnp.where(chosen, 1.0, 0.0).astype(BF16)
+    mix = jnp.where(chosen, share, 0.0)
+    mix_high = mix.astype(BF16)
+    mix_low = (mix - mix_high.astype(F32)).astype(BF16)
+
+    own = jnp.zeros((tokens, 1), F32)
+    for f in range(2):
+        part_copy(f).wait_recv()
+        at = pl.ds(f * wide, wide)
+        state = resid[:, at].astype(F32) + (acc[f, :tokens, :] + part_in[f].astype(F32))
+        hidden_buf[:, at] = state
+        own += jnp.sum(state * state, axis=1, keepdims=True)
+    squares[...] = jnp.broadcast_to(own, squares.shape)
+    sq = pltpu.make_async_remote_copy(
+        src_ref=squares, dst_ref=peer_squares, send_sem=sq_sem.at[0], recv_sem=sq_sem.at[1],
+        device_id=(c, 1 - e), device_id_type=MESH,
+    )
+    sq.start()
+    sq.wait()
+    mean = (squares[:, :1] + peer_squares[:, :1]) / D
+    normed = (hidden_buf[...] * lax.rsqrt(mean + epsilon) * gain_ref[...]).astype(BF16)
+    two[:tokens, :] = normed
+    for j in range(blocks // 2):
+        sent = lax.dot_general(
+            pick, two[:tokens, j * 256 : (j + 1) * 256], (((0,), (0,)), ((), ())),
+            preferred_element_type=F32,
+        )
+        stage[pl.ds(2 * j, rows, stride=blocks), :] = sent[:, :128]
+        stage[pl.ds(2 * j + 1, rows, stride=blocks), :] = sent[:, 128:]
+    outbox[...] = stage[...].reshape(outbox.shape).astype(BF16)
+
+    def a_copy(j):
+        to = (c + j) % n
+        return pltpu.make_async_remote_copy(
+            src_ref=outbox.at[to], dst_ref=inbox.at[c], send_sem=a_send.at[j],
+            recv_sem=a_recv.at[c], device_id=(to, e), device_id_type=MESH,
+        )
+
+    def b_copy(j):
+        to = (c + j) % n
+        return pltpu.make_async_remote_copy(
+            src_ref=backbox.at[to], dst_ref=endbox.at[c], send_sem=b_send.at[j],
+            recv_sem=b_recv.at[c], device_id=(to, e), device_id_type=MESH,
+        )
+
+    def arrived(box, sems):
+        @pl.loop(1, n)
+        def _(j):
+            source = (c + j) % n
+            pltpu.make_async_remote_copy(
+                src_ref=box.at[source], dst_ref=box.at[source], send_sem=a_send.at[0],
+                recv_sem=sems.at[source], device_id=(source, e), device_id_type=MESH,
+            ).wait_recv()
+
+        stage[...] = box[...].reshape(stage.shape).astype(F32)
+        for j in range(blocks):
+            two[:, j * 128 : (j + 1) * 128] = stage[pl.ds(j, rows, stride=blocks), :].astype(BF16)
+
+    @pl.loop(1, n)
+    def _(j):
+        a_copy(j).start()
+
+    inbox[c] = outbox[c]
+    unpack(3 * (n_unpack // 4), n_unpack // 4)
+    arrived(inbox, a_recv)
+    width = parts.shape[3]
+
+    def p_copy(m):
+        return pltpu.make_async_remote_copy(
+            src_ref=parts.at[m], dst_ref=peer_parts.at[m], send_sem=p_send.at[m],
+            recv_sem=p_recv.at[m], device_id=(c, 1 - e), device_id_type=MESH,
+        )
+
+    n_parts = units // width
+    for m in range(n_parts):
+        for side in range(2):
+            start = side * units + m * width
+            parts[m, side] = jnp.dot(
+                two[...], gu[:, start : start + width], preferred_element_type=F32
+            ).astype(BF16)
+        p_copy(m).start()
+    for m in range(n_parts):
+        p_copy(m).wait_recv()
+        gate = parts[m, 0].astype(F32) + peer_parts[m, 0].astype(F32)
+        up = parts[m, 1].astype(F32) + peer_parts[m, 1].astype(F32)
+        act[:, m * width : (m + 1) * width] = (gate / (1.0 + jnp.exp(-gate)) * up).astype(BF16)
+    load_down.wait()
+    for j in range(blocks // 2):
+        result = jnp.dot(
+            act[...], down[:, j * 256 : (j + 1) * 256], preferred_element_type=F32
+        )
+        stage[pl.ds(2 * j, rows, stride=blocks), :] = result[:, :128]
+        stage[pl.ds(2 * j + 1, rows, stride=blocks), :] = result[:, 128:]
+    backbox[...] = stage[...].reshape(backbox.shape).astype(BF16)
+
+    @pl.loop(1, n)
+    def _(j):
+        b_copy(j).start()
+
+    endbox[c] = backbox[c]
+    arrived(endbox, b_recv)
+    routed = jnp.dot(mix_high, two[...], preferred_element_type=F32)
+    routed += jnp.dot(mix_low, two[...], preferred_element_type=F32)
+    mixed_ref[...] = (hidden_buf[...] + routed).astype(BF16)
+
+    for slot_index in range(15):
+        kv_copy(c, slot_index, sibling).wait_send()
+    for f in range(2):
+        swap(f).wait_send()
+        part_copy(f).wait_send()
+    to_partner.wait_send()
+    own_over.wait_send()
+    partner_over.wait_send()
+
+    @pl.loop(0, 2)
+    def _(g):
+        w_copy(mine, 0, g, fwd_y.at[g], sibling).wait_send()
+        w_copy(mine, 0, g, fwd_z.at[g], sibling).wait_send()
+        for f in range(2):
+            w_copy(mine, f, g, own_z.at[f, g], sibling).wait_send()
+            w_copy(mine, f, g, own_y.at[f, g], sibling).wait_send()
+            for source in range(4):
+                w_copy(mine, f, g, w_sib.at[source, f, g], sibling).wait_send()
+
+    @pl.loop(1, n)
+    def _(j):
+        a_copy(j).wait_send()
+        b_copy(j).wait_send()
+
+    for m in range(n_parts):
+        p_copy(m).wait_send()
+
+
+def fast_body(queries, keys, values, resid, gain, expert_ids, gate_scores, w_gate_up, w_down, w_out):
+    tokens, heads, size = queries.shape
+    n = lax.axis_size("ctx")
+    half = resid.shape[1]
+    wide = half // 2
+    capacity = max(2, 5 * tokens * TOPK // (4 * EXPERTS))
+    depth = heads * w_out.shape[1]
+    units = w_down.shape[1]
+    rows = n * capacity
+    blocks = half // 128
+    box = (n, capacity, blocks, 128)
+    width = 256
+    vmem = pl.BlockSpec(memory_space=pltpu.VMEM)
+    hbm = pl.BlockSpec(memory_space=pl.ANY)
+    dma = pltpu.SemaphoreType.DMA
+    context, mixed = pl.pallas_call(
+        layer_kernel,
+        out_shape=(
+            jax.ShapeDtypeStruct((tokens * heads, size), BF16),
+            jax.ShapeDtypeStruct((tokens, half), BF16),
+        ),
+        in_specs=[hbm, vmem, vmem, hbm, hbm, vmem, vmem, vmem, hbm, hbm],
+        out_specs=(vmem, vmem),
+        scratch_shapes=[
+            pltpu.VMEM((tokens * heads, size), BF16),
+            pltpu.VMEM((tokens, half), BF16),
+            pltpu.VMEM((n, 2 * tokens, size), BF16),
+            pltpu.VMEM((2, HALF_Z, 2, depth, wide), BF16),
+            pltpu.VMEM((tokens * heads, size), F32),
+            pltpu.VMEM((tokens, heads * size), BF16),
+            pltpu.VMEM((3, 2, HALF_Z // 2, tokens, 2 * depth), BF16),
+            pltpu.VMEM((heads * size, 2 * depth), jnp.int32),
+            pltpu.VMEM((2, 2 * tokens, wide), F32),
+            pltpu.VMEM((2, tokens, wide), BF16),
+            pltpu.VMEM((2, tokens, wide), BF16),
+            pltpu.VMEM((half, 2, units), BF16),
+            pltpu.VMEM((half, 2 * units), BF16),
+            pltpu.VMEM((units, half), BF16),
+            pltpu.VMEM((tokens, 128), F32),
+            pltpu.VMEM((tokens, 128), F32),
+            pltpu.VMEM((tokens, half), F32),
+            pltpu.VMEM((rows * blocks, 128), F32),
+            pltpu.VMEM((rows, half), BF16),
+            pltpu.VMEM(box, BF16), pltpu.VMEM(box, BF16), pltpu.VMEM(box, BF16), pltpu.VMEM(box, BF16),
+            pltpu.VMEM((units // width, 2, rows, width), BF16),
+            pltpu.VMEM((units // width, 2, rows, width), BF16),
+            pltpu.VMEM((rows, units), BF16),
+            dma((15,)), dma((n,)), dma((2, 2)), dma((2,)), dma((2, 2)), dma((2,)),
+            dma((4, 2, 2)), dma((HALF_Z, 2, 2)), dma((2,)), dma((3,)), dma((3,)), dma((2,)), dma((2,)),
+            dma((2,)), dma((units // width,)), dma((units // width,)),
+            dma((n,)), dma((n,)), dma((n,)), dma((n,)), dma((6,)),
+        ],
+        compiler_params=pltpu.CompilerParams(
+            collective_id=0, has_side_effects=True, vmem_limit_bytes=56 * 2**20
+        ),
+        name="layer",
+    )(
+        queries.reshape(tokens * heads, size), keys.reshape(tokens, -1), values.reshape(tokens, -1),
+        w_out.reshape(depth, 2 * half), resid, gain.reshape(1, half), expert_ids, gate_scores,
+        w_gate_up[0], w_down[0],
+    )
+    return (context.reshape(tokens, heads, size), mixed)
+
+
 def solution(mesh):
     in_specs = (
         P("ctx", "exp", None),
@@ -157,4 +657,6 @@
         P("exp", "ctx", None),
     )
     out_specs = (P("ctx", "exp", None), P("ctx", "exp"))
+    fits = mesh.shape["ctx"] == N_Z * PLANE and mesh.shape["exp"] == 2
+    body = fast_body if fits else general_body
     return jax.shard_map(body, mesh=mesh, in_specs=in_specs, out_specs=out_specs, check_vma=False)

time: 314 us -> 134 us (0.43)
  waiting for transfers between devices: 128 us -> 0 us
  Pallas kernels: 0 us -> 123 us
  blocking collectives: 87.2 us -> 0 us
  matrix products: 28.2 us -> 0 us
  other arithmetic: 27.1 us -> 0 us
  between operations: 14.6 us -> 0.64 us
  local copies, waits for them, and re-layouts: 21.8 us -> 8.11 us
  starting transfers between devices: 6.32 us -> 0 us
    pallas_call x0 -> x1, Pallas kernels: none -> 123 us  [fast_body(): pl.pallas_call(layer_kernel, out_shape=(jax.ShapeDtypeStruct((tokens * he...]
    all_gather x1 -> x0, waiting for transfers between devices: 64.7 us -> none  [body(): whole_out = lax.all_gather(w_out, 'ctx', axis=1, tiled=True)]
    all_gather x2 -> x0, blocking collectives: 50.7 us -> none  [the longest x1 27.4 us: body(): lax.all_gather(key_local, 'ctx', axis=0, tiled=True)]
    all_to_all x1 -> x0, blocking collectives: 32.7 us -> none  [body(): lax.all_to_all(outgoing, 'ctx', split_axis=0, concat_axis=0, tiled=True)]
    dot_general x6 -> x0, matrix products: 28.2 us -> none  [the longest x1 9.29 us: body(): jnp.einsum('thp,hpd->td', context, whole_out, preferred_element_type=jnp....]
    psum x1 -> x0, waiting for transfers between devices: 26.5 us -> none  [body(): lax.psum(partial_sum.astype(jnp.bfloat16), 'exp').astype(jnp.float32)]
    all_to_all x1 -> x0, waiting for transfers between devices: 23 us -> none  [body(): lax.all_to_all(result, 'ctx', split_axis=0, concat_axis=0, tiled=True)]
    reduce_scatter x1 -> x0, waiting for transfers between devices: 12.7 us -> none  [body(): lax.psum_scatter(projected.astype(jnp.bfloat16), 'exp', scatter_dimension...]
  transfers between devices with their start and end apart: 4 -> 0, of which waited for: 4 -> 0; matrix products, arithmetic and copies ran while one was open for 8% -> 0% of each run, Pallas kernels for 0% -> 0%
where the time goes in v2:
time: 134 us; the launch traced here: 132 us
  Pallas kernels  123 us (92%)
  local copies, waits for them, and re-layouts  8.11 us (6%)
    pallas_call x1, Pallas kernels, fast_body(): pl.pallas_call(layer_kernel, out_shape=(jax.ShapeDtypeStruct((tokens * he...  123 us
    unnamed x4, local copies, waits for them, and re-layouts  6.57 us

profile of v2, /device:TPU:1, one launch (start us, length us, event | category | flops | bytes accessed | tf_op | source)
XLA Modules:
  0.0 131.8 jit_solution(8159917329125540731)
XLA Ops:
  0.6 1.4 %copy.12.ids_ref = s32[128,8]{1,0:T(8,128)} copy(s32[128,8]{0,1:T(8,128)} %param.15) | data formatting | bytes 8192 | tf_op args[5]
  2.0 1.4 %copy.13.gate_ref = f32[128,8]{1,0:T(8,128)} copy(f32[128,8]{0,1:T(8,128)} %param.16) | data formatting | bytes 8192 | tf_op args[6]
  3.5 1.5 %copy_bitcast_fusion = (bf16[128,256]{1,0:T(8,128)(2,1)}, bf16[128,256]{1,0:T(8,128)(2,1)}) fusion(bf16[16,8,2,128]{3,2,1,0:T(2,128)(2,1)} %bitcast.17, bf16[16,8,2,128]{3,2,1,0:T(2,128)(2,1)} %bitcast.18), kind=kLoop, calls=%fused_computation | loop fusion | bytes 262144 | tf_op jit(solution)/shard_map/reshape | solution.py:639
  5.0 123.1 %layer.1 = (bf16[2048,128]{1,0:T(8,128)(2,1)}, bf16[128,2048]{1,0:T(8,128)(2,1)}) custom-call(bf16[2048,128]{1,0:T(8,128)(2,1)} %bitcast.15, bf16[128,256]{1,0:T(8,128)(2,1)} %get-tuple-element.7.key_ref, bf16[128,256]{1,0:T(8,128)(2,1)} %get-tuple-element.6.value_ref, bf16[128,4096]{1,0:T(8,128)(2,1)} %bitcast.14, bf16[128,2048]{1,0:T(8,128)(2,1)} %resid_hbm.1, ...), custom_call_target="tpu_custom_call" | custom-call | tf_op jit(solution)/shard_map/layer/pallas_call | solution.py:597
  128.1 1.9 %copy.20 = bf16[128,16,128]{2,1,0:T(8,128)(2,1)} copy(bf16[128,16,128]{2,1,0:T(8,128)(2,1)} %bitcast.16) | data formatting | bytes 1048576
  129.9 1.9 %copy.21 = bf16[128,2048]{1,0:T(8,128)(2,1)} copy(bf16[128,2048]{1,0:T(8,128)(2,1)} %get-tuple-element.11) | data formatting | bytes 1048576

commit v3 on v2

--- a/solution.py
+++ b/solution.py
@@ -155,11 +155,11 @@
 
 
 def layer_kernel(
-    q_hbm, key_ref, value_ref, w_hbm, resid_hbm, gain_ref, ids_ref, gate_ref, gu_hbm, down_hbm,
+    q_hbm, key_hbm, value_hbm, w_hbm, resid_hbm, gain_hbm, ids_hbm, gate_hbm, gu_hbm, down_hbm,
     ctx_ref, mixed_ref,
-    q_in, resid, kvbuf, wbuf, rows32, ctx2d, ctxbuf, target, acc, part_out, part_in,
+    key_ref, value_ref, gain_ref, ids_ref, gate_ref, q_in, resid, kvbuf, wbuf, rows32, ctx2d, ctxbuf, target, acc, part_out, part_in,
     gu_raw, gu, down, squares, peer_squares, hidden_buf, stage, two, outbox, inbox, backbox, endbox,
-    parts, peer_parts, act,
+    parts, peer_parts, act, mixes, normed_buf,
     kv_send, kv_recv, own_z, fwd_z, own_y, fwd_y, w_sib, w_recv, x_send, c_send, c_recv, h_send, h_recv,
     sq_sem, p_send, p_recv, a_send, a_recv, b_send, b_recv, local_sem,
 ):
@@ -210,15 +210,29 @@
     load_resid = pltpu.make_async_copy(resid_hbm, resid, local_sem.at[3])
     load_gu = pltpu.make_async_copy(gu_hbm, gu_raw, local_sem.at[4])
     load_down = pltpu.make_async_copy(down_hbm, down, local_sem.at[5])
+    small = [
+        pltpu.make_async_copy(source, held, local_sem.at[6 + i])
+        for i, (source, held) in enumerate(
+            (
+                (key_hbm, key_ref), (value_hbm, value_ref), (gain_hbm, gain_ref),
+                (ids_hbm, ids_ref), (gate_hbm, gate_ref),
+            )
+        )
+    ]
+    for copy in small:
+        copy.start()
     own_load(0).start()
     own_load(1).start()
     load_q.start()
     load_resid.start()
     load_gu.start()
     load_down.start()
-    lane = pl.ds(pl.multiple_of(e * 128, 128), 128)
-    kvbuf[c, :tokens, :] = key_ref[:, lane]
-    kvbuf[c, tokens:, :] = value_ref[:, lane]
+    small[0].wait()
+    small[1].wait()
+    group = e * heads // (HQ // KVH)
+    for part, source in enumerate((key_ref, value_ref)):
+        picked = jnp.where(group == 0, source[:, 0, :].astype(F32), source[:, 1, :].astype(F32))
+        kvbuf[c, part * tokens : (part + 1) * tokens, :] = picked.astype(BF16)
     pl.semaphore_wait(barrier, n)
 
     def kv_copy(block, slot, to):
@@ -258,8 +272,6 @@
     kv_copy(c, 7, sibling).start()
     swap(0).start()
     swap(1).start()
-    own_load(0).wait()
-    send_own(0, 0)
     load_q.wait()
     rows32[...] = q_in[...].astype(F32)
     for step in range(1, N_Z):
@@ -267,6 +279,8 @@
         kv_copy(block, 0, sibling).wait_recv()
         kv_copy(block, 3 + step, y_peer).start()
         kv_copy(block, 7 + step, sibling).start()
+    own_load(0).wait()
+    send_own(0, 0)
     wait_block(mine, 0, group_of(1))
     send_own(0, 1)
     own_load(1).wait()
@@ -277,14 +291,15 @@
         block = ((z + step) % N_Z) * PLANE + (1 - y) * 2 + k
         kv_copy(block, 0, sibling).wait_recv()
         kv_copy(block, 11 + step, sibling).start()
+    depth_part = depth // 2
     row = lax.broadcasted_iota(jnp.int32, target.shape, 0)
     col = lax.broadcasted_iota(jnp.int32, target.shape, 1)
-    target[...] = row - ((col % 128) // 8) * 128 - (col // 128) * 8 - col % 8
+    target[...] = row - ((col % depth_part) // 8) * 128 - (col // depth_part) * 8 - col % 8
     for block_z in range(N_Z):
         for block_y in range(2):
             kv_copy(block_z * PLANE + block_y * 2 + 1 - k, 0, sibling).wait_recv()
 
-    scale = 1.0 / math.sqrt(q_in.shape[1])
+    scale = math.log2(math.e) / math.sqrt(q_in.shape[1])
     n_keys = n * tokens
 
     def attend(pair):
@@ -295,25 +310,59 @@
         value_all = kvbuf[:, tokens:, :].reshape(n_keys, 128)
         scores = lax.dot_general(
             both, key_all, (((1,), (1,)), ((), ())), preferred_element_type=F32
-        ) * scale
+        )
         q_pos = c * tokens + lax.broadcasted_iota(jnp.int32, scores.shape, 0) % tokens
         k_pos = lax.broadcasted_iota(jnp.int32, scores.shape, 1)
         masked = jnp.where(k_pos <= q_pos, scores, masked_score)
         best = jnp.max(masked, axis=1, keepdims=True)
-        prob = jnp.exp(masked - best)
+        prob = jnp.exp2((masked - best) * scale)
         total = jnp.sum(prob, axis=1, keepdims=True)
         part = jnp.dot(prob.astype(BF16), value_all, preferred_element_type=F32)
         done = (part / total).astype(BF16)
-        ctx2d[:, pl.ds(pl.multiple_of(pair * 256, 256), 128)] = done[:tokens]
-        ctx2d[:, pl.ds(pl.multiple_of(pair * 256 + 128, 128), 128)] = done[tokens:]
+        turn = pair // (heads // 4)
+        at = pair % (heads // 4) * 256
+        ctx2d[turn, :, pl.ds(pl.multiple_of(at, 256), 128)] = done[:tokens]
+        ctx2d[turn, :, pl.ds(pl.multiple_of(at + 128, 128), 128)] = done[tokens:]
         rows32[pl.ds(2 * pair, tokens, stride=heads), :] = done[:tokens].astype(F32)
         rows32[pl.ds(2 * pair + 1, tokens, stride=heads), :] = done[tokens:].astype(F32)
+
+    def ctx_copy(slot, hh, src, dst, to):
+        return pltpu.make_async_remote_copy(
+            src_ref=src, dst_ref=dst, send_sem=c_send.at[slot, hh], recv_sem=c_recv.at[slot, hh],
+            device_id=to, device_id_type=MESH,
+        )
+
+    def to_partner(hh):
+        return ctx_copy(0, hh, ctxbuf.at[2, 0, hh], ctxbuf.at[1, e, hh], (partner, e))
+
+    def over(slot, hh):
+        return ctx_copy(1 + slot, hh, ctxbuf.at[slot, e, hh], ctxbuf.at[slot, e, hh], (c, 1 - e))
+
+    def pass_on(hh):
+        ctx_copy(0, hh, ctxbuf.at[1, e, hh], ctxbuf.at[1, e, hh], (partner, e)).wait_recv()
+        over(1, hh).start()
+
+    def pick_quad(hh, quad):
+        pick = jnp.where(target[...] == 32 * quad, 1.0, 0.0).astype(BF16)
+        return jnp.dot(ctx2d[hh], pick, preferred_element_type=F32).astype(BF16)
 
     @pl.loop(0, 2)
     def _(turn):
         @pl.loop(0, heads // 4)
         def _(step):
             attend(turn * (heads // 4) + step)
+
+        @pl.loop(0, 2)
+        def _(quad):
+            ctxbuf[2, 0, turn, quad] = pick_quad(turn, (1 - zh) * 2 + quad)
+
+        to_partner(turn).start()
+
+        @pl.loop(0, 2)
+        def _(quad):
+            ctxbuf[0, e, turn, quad] = pick_quad(turn, zh * 2 + quad)
+
+        over(0, turn).start()
 
         @pl.when(turn == 0)
         def _():
@@ -326,31 +375,7 @@
                 wait_block(block_of(0, 1, 0), 0, g)
                 w_copy(block_of(0, 1, 0), 0, g, w_sib.at[2, 0, g], sibling).start()
 
-    def pick_pair(pair):
-        pick = jnp.where(target[...] == 16 * pair, 1.0, 0.0).astype(BF16)
-        return jnp.dot(ctx2d[...], pick, preferred_element_type=F32).astype(BF16)
-
-    n_pairs = ctxbuf.shape[2]
-
-    @pl.loop(0, n_pairs)
-    def _(pair):
-        ctxbuf[2, 0, pair] = pick_pair((1 - zh) * n_pairs + pair)
-
-    def ctx_copy(slot, src, dst, to):
-        return pltpu.make_async_remote_copy(
-            src_ref=src, dst_ref=dst, send_sem=c_send.at[slot], recv_sem=c_recv.at[slot],
-            device_id=to, device_id_type=MESH,
-        )
-
-    to_partner = ctx_copy(0, ctxbuf.at[2, 0], ctxbuf.at[1, e], (partner, e))
-    to_partner.start()
-
-    @pl.loop(0, n_pairs)
-    def _(pair):
-        ctxbuf[0, e, pair] = pick_pair(zh * n_pairs + pair)
-
-    own_over = ctx_copy(1, ctxbuf.at[0, e], ctxbuf.at[0, e], (c, 1 - e))
-    own_over.start()
+    pass_on(0)
 
     @pl.loop(0, 2)
     def _(s):
@@ -374,12 +399,7 @@
     n_unpack = half // unpack_rows
     load_gu.wait()
     unpack(0, n_unpack // 4)
-    pltpu.make_async_remote_copy(
-        src_ref=ctxbuf.at[1, e], dst_ref=ctxbuf.at[1, e], send_sem=c_send.at[0],
-        recv_sem=c_recv.at[0], device_id=(partner, e), device_id_type=MESH,
-    ).wait_recv()
-    partner_over = ctx_copy(2, ctxbuf.at[1, e], ctxbuf.at[1, e], (c, 1 - e))
-    partner_over.start()
+    pass_on(1)
 
     def relay_far(f):
         @pl.loop(0, 2)
@@ -392,24 +412,26 @@
     unpack(n_unpack // 4, n_unpack // 4)
     ctx_ref[...] = rows32[...].astype(BF16)
     acc[...] = jnp.zeros_like(acc)
-    for slot in range(2):
-        pltpu.make_async_remote_copy(
-            src_ref=ctxbuf.at[slot, 1 - e], dst_ref=ctxbuf.at[slot, 1 - e], send_sem=c_send.at[0],
-            recv_sem=c_recv.at[1 + slot], device_id=(c, 1 - e), device_id_type=MESH,
-        ).wait_recv()
+    for hh in range(2):
+        for slot in range(2):
+            ctx_copy(
+                1 + slot, hh, ctxbuf.at[slot, 1 - e, hh], ctxbuf.at[slot, 1 - e, hh], (c, 1 - e)
+            ).wait_recv()
 
     def project(f):
-        @pl.loop(0, 8)
+        @pl.loop(0, 4)
         def _(i):
-            other_z = i // 4
-            other_y = (i // 2) % 2
+            other_z = i // 2
             g = group_of(i % 2)
-            wait_block(block_of(other_z, other_y, 1), f, g)
-            first = block_of(other_z, other_y, 0)
-            pair = first // 2
-            weights = wbuf[f, pl.ds(2 * pair, 2), pl.ds(g, 1)].reshape(2 * depth, wide)
-            lhs = jnp.concatenate([ctxbuf[0, g, pair], ctxbuf[1, g, pair]], axis=0)
-            acc[f] += jnp.dot(lhs, weights, preferred_element_type=F32)
+            wait_block(block_of(other_z, 0, 1), f, g)
+            wait_block(block_of(other_z, 1, 1), f, g)
+            quad = zl + other_z * (1 - 2 * zl)
+            for hh in range(2):
+                weights = wbuf[
+                    f, pl.ds(quad * PLANE, PLANE), pl.ds(g, 1), hh * depth_part : (hh + 1) * depth_part
+                ].reshape(PLANE * depth_part, wide)
+                lhs = jnp.concatenate([ctxbuf[0, g, hh, quad], ctxbuf[1, g, hh, quad]], axis=0)
+                acc[f] += jnp.dot(lhs, weights, preferred_element_type=F32)
 
         part_out[f] = acc[f, tokens:, :].astype(BF16)
         pltpu.make_async_remote_copy(
@@ -429,27 +451,30 @@
     load_resid.wait()
     unpack(n_unpack // 2, n_unpack // 4)
 
-    slot = lax.broadcasted_iota(jnp.int32, (tokens, rows), 1)
-    named = jnp.zeros((tokens, rows), F32)
-    share = jnp.zeros((tokens, rows), F32)
+    for copy in small[2:]:
+        copy.wait()
+    slot = lax.broadcasted_iota(jnp.int32, (rows, tokens), 0)
+    named = jnp.zeros((rows, tokens), F32)
+    share = jnp.zeros((rows, tokens), F32)
     gates = gate_ref[...]
-    gates = gates / jnp.sum(gates, axis=1, keepdims=True)
+    gates = gates / jnp.sum(gates, axis=0, keepdims=True)
     for column in range(TOPK):
-        hit = ids_ref[:, column : column + 1] == slot // cap
+        hit = ids_ref[column : column + 1, :] == slot // cap
         named = jnp.where(hit, 1.0, named)
-        share = jnp.where(hit, gates[:, column : column + 1], share)
+        share = jnp.where(hit, gates[column : column + 1, :], share)
     before = jnp.where(
-        lax.broadcasted_iota(jnp.int32, (tokens, tokens), 1)
-        < lax.broadcasted_iota(jnp.int32, (tokens, tokens), 0),
+        lax.broadcasted_iota(jnp.int32, (tokens, tokens), 0)
+        < lax.broadcasted_iota(jnp.int32, (tokens, tokens), 1),
         1.0,
         0.0,
     ).astype(BF16)
-    rank = jnp.dot(before, named.astype(BF16), preferred_element_type=F32)
+    rank = jnp.dot(named.astype(BF16), before, preferred_element_type=F32)
     chosen = jnp.logical_and(named > 0.5, rank == (slot % cap).astype(F32))
-    pick = jnp.where(chosen, 1.0, 0.0).astype(BF16)
+    pick_all = jnp.where(chosen, 1.0, 0.0).astype(BF16)
     mix = jnp.where(chosen, share, 0.0)
     mix_high = mix.astype(BF16)
-    mix_low = (mix - mix_high.astype(F32)).astype(BF16)
+    mixes[0] = mix_high
+    mixes[1] = (mix - mix_high.astype(F32)).astype(BF16)
 
     own = jnp.zeros((tokens, 1), F32)
     for f in range(2):
@@ -467,98 +492,136 @@
     sq.wait()
     mean = (squares[:, :1] + peer_squares[:, :1]) / D
     normed = (hidden_buf[...] * lax.rsqrt(mean + epsilon) * gain_ref[...]).astype(BF16)
-    two[:tokens, :] = normed
+    normed_buf[...] = normed
     for j in range(blocks // 2):
-        sent = lax.dot_general(
-            pick, two[:tokens, j * 256 : (j + 1) * 256], (((0,), (0,)), ((), ())),
-            preferred_element_type=F32,
+        sent = jnp.dot(
+            pick_all, normed_buf[:, j * 256 : (j + 1) * 256], preferred_element_type=F32
         )
         stage[pl.ds(2 * j, rows, stride=blocks), :] = sent[:, :128]
         stage[pl.ds(2 * j + 1, rows, stride=blocks), :] = sent[:, 128:]
     outbox[...] = stage[...].reshape(outbox.shape).astype(BF16)
 
-    def a_copy(j):
-        to = (c + j) % n
+    def a_copy(to):
         return pltpu.make_async_remote_copy(
-            src_ref=outbox.at[to], dst_ref=inbox.at[c], send_sem=a_send.at[j],
+            src_ref=outbox.at[to], dst_ref=inbox.at[c], send_sem=a_send.at[to],
             recv_sem=a_recv.at[c], device_id=(to, e), device_id_type=MESH,
         )
 
-    def b_copy(j):
-        to = (c + j) % n
+    def b_copy(to):
         return pltpu.make_async_remote_copy(
-            src_ref=backbox.at[to], dst_ref=endbox.at[c], send_sem=b_send.at[j],
+            src_ref=backbox.at[to], dst_ref=endbox.at[c], send_sem=b_send.at[to],
             recv_sem=b_recv.at[c], device_id=(to, e), device_id_type=MESH,
         )
 
-    def arrived(box, sems):
-        @pl.loop(1, n)
+    near_rows = rows // 2
+    near_n = n // 2
+
+    def half_of(t):
+        return zh + t * (1 - 2 * zh)
+
+    def from_half(box, sems, t):
+        first = half_of(t) * near_n
+
+        @pl.loop(0, near_n)
         def _(j):
-            source = (c + j) % n
-            pltpu.make_async_remote_copy(
-                src_ref=box.at[source], dst_ref=box.at[source], send_sem=a_send.at[0],
-                recv_sem=sems.at[source], device_id=(source, e), device_id_type=MESH,
-            ).wait_recv()
-
-        stage[...] = box[...].reshape(stage.shape).astype(F32)
+            source = first + j
+
+            @pl.when(source != c)
+            def _():
+                pltpu.make_async_remote_copy(
+                    src_ref=box.at[source], dst_ref=box.at[source], send_sem=a_send.at[0],
+                    recv_sem=sems.at[source], device_id=(source, e), device_id_type=MESH,
+                ).wait_recv()
+
+        part_stage = stage.at[pl.ds(0, near_rows * blocks)]
+        part_stage[...] = box[pl.ds(first, near_n)].reshape(near_rows * blocks, 128).astype(F32)
         for j in range(blocks):
-            two[:, j * 128 : (j + 1) * 128] = stage[pl.ds(j, rows, stride=blocks), :].astype(BF16)
-
-    @pl.loop(1, n)
-    def _(j):
-        a_copy(j).start()
-
+            two[t, :, j * 128 : (j + 1) * 128] = stage[
+                pl.ds(j, near_rows, stride=blocks), :
+            ].astype(BF16)
+
+    def far_first(start):
+        @pl.loop(0, near_n)
+        def _(j):
+            start((1 - zh) * near_n + (c + j) % near_n)
+
+        @pl.loop(1, near_n)
+        def _(j):
+            start(zh * near_n + (c + j) % near_n)
+
+    far_first(lambda to: a_copy(to).start())
     inbox[c] = outbox[c]
     unpack(3 * (n_unpack // 4), n_unpack // 4)
-    arrived(inbox, a_recv)
-    width = parts.shape[3]
-
-    def p_copy(m):
+    width = parts.shape[4]
+
+    def p_copy(t, m):
         return pltpu.make_async_remote_copy(
-            src_ref=parts.at[m], dst_ref=peer_parts.at[m], send_sem=p_send.at[m],
-            recv_sem=p_recv.at[m], device_id=(c, 1 - e), device_id_type=MESH,
+            src_ref=parts.at[t, m], dst_ref=peer_parts.at[t, m], send_sem=p_send.at[t, m],
+            recv_sem=p_recv.at[t, m], device_id=(c, 1 - e), device_id_type=MESH,
         )
 
     n_parts = units // width
-    for m in range(n_parts):
-        for side in range(2):
-            start = side * units + m * width
-            parts[m, side] = jnp.dot(
-                two[...], gu[:, start : start + width], preferred_element_type=F32
-            ).astype(BF16)
-        p_copy(m).start()
-    for m in range(n_parts):
-        p_copy(m).wait_recv()
-        gate = parts[m, 0].astype(F32) + peer_parts[m, 0].astype(F32)
-        up = parts[m, 1].astype(F32) + peer_parts[m, 1].astype(F32)
-        act[:, m * width : (m + 1) * width] = (gate / (1.0 + jnp.exp(-gate)) * up).astype(BF16)
+
+    @pl.loop(0, 2)
+    def _(t):
+        from_half(inbox, a_recv, t)
+        for m in range(n_parts):
+            for side in range(2):
+                start = side * units + m * width
+                parts[t, m, side] = jnp.dot(
+                    two[t], gu[:, start : start + width], preferred_element_type=F32
+                ).astype(BF16)
+            p_copy(t, m).start()
+
     load_down.wait()
-    for j in range(blocks // 2):
-        result = jnp.dot(
-            act[...], down[:, j * 256 : (j + 1) * 256], preferred_element_type=F32
-        )
-        stage[pl.ds(2 * j, rows, stride=blocks), :] = result[:, :128]
-        stage[pl.ds(2 * j + 1, rows, stride=blocks), :] = result[:, 128:]
-    backbox[...] = stage[...].reshape(backbox.shape).astype(BF16)
-
-    @pl.loop(1, n)
-    def _(j):
-        b_copy(j).start()
+
+    @pl.loop(0, 2)
+    def _(t):
+        for m in range(n_parts):
+            p_copy(t, m).wait_recv()
+            gate = parts[t, m, 0].astype(F32) + peer_parts[t, m, 0].astype(F32)
+            up = parts[t, m, 1].astype(F32) + peer_parts[t, m, 1].astype(F32)
+            act[:, m * width : (m + 1) * width] = (gate / (1.0 + jnp.exp(-gate)) * up).astype(BF16)
+        for j in range(blocks // 2):
+            result = jnp.dot(
+                act[...], down[:, j * 256 : (j + 1) * 256], preferred_element_type=F32
+            )
+            stage[pl.ds(2 * j, near_rows, stride=blocks), :] = result[:, :128]
+            stage[pl.ds(2 * j + 1, near_rows, stride=blocks), :] = result[:, 128:]
+        first = half_of(t) * near_n
+        backbox[pl.ds(first, near_n)] = (
+            stage[: near_rows * blocks, :].reshape((near_n,) + backbox.shape[1:]).astype(BF16)
+        )
+
+        @pl.loop(0, near_n)
+        def _(j):
+            to = first + (c + j) % near_n
+
+            @pl.when(to != c)
+            def _():
+                b_copy(to).start()
 
     endbox[c] = backbox[c]
-    arrived(endbox, b_recv)
-    routed = jnp.dot(mix_high, two[...], preferred_element_type=F32)
-    routed += jnp.dot(mix_low, two[...], preferred_element_type=F32)
-    mixed_ref[...] = (hidden_buf[...] + routed).astype(BF16)
+
+    @pl.loop(0, 2)
+    def _(t):
+        from_half(endbox, b_recv, t)
+        at = pl.ds(pl.multiple_of(half_of(t) * near_rows, 16), near_rows)
+        for part in range(2):
+            hidden_buf[...] += lax.dot_general(
+                mixes[part, at, :], two[t], (((0,), (0,)), ((), ())), preferred_element_type=F32
+            )
+
+    mixed_ref[...] = hidden_buf[...].astype(BF16)
 
     for slot_index in range(15):
         kv_copy(c, slot_index, sibling).wait_send()
     for f in range(2):
         swap(f).wait_send()
         part_copy(f).wait_send()
-    to_partner.wait_send()
-    own_over.wait_send()
-    partner_over.wait_send()
+        to_partner(f).wait_send()
+        over(0, f).wait_send()
+        over(1, f).wait_send()
 
     @pl.loop(0, 2)
     def _(g):
@@ -572,11 +635,12 @@
 
     @pl.loop(1, n)
     def _(j):
-        a_copy(j).wait_send()
-        b_copy(j).wait_send()
-
-    for m in range(n_parts):
-        p_copy(m).wait_send()
+        a_copy((c + j) % n).wait_send()
+        b_copy((c + j) % n).wait_send()
+
+    for t in range(2):
+        for m in range(n_parts):
+            p_copy(t, m).wait_send()
 
 
 def fast_body(queries, keys, values, resid, gain, expert_ids, gate_scores, w_gate_up, w_down, w_out):
@@ -592,7 +656,7 @@
     box = (n, capacity, blocks, 128)
     width = 256
     vmem = pl.BlockSpec(memory_space=pltpu.VMEM)
-    hbm = pl.BlockSpec(memory_space=pl.ANY)
+    hbm = pl.BlockSpec(memory_space=pltpu.HBM)
     dma = pltpu.SemaphoreType.DMA
     context, mixed = pl.pallas_call(
         layer_kernel,
@@ -600,17 +664,19 @@
             jax.ShapeDtypeStruct((tokens * heads, size), BF16),
             jax.ShapeDtypeStruct((tokens, half), BF16),
         ),
-        in_specs=[hbm, vmem, vmem, hbm, hbm, vmem, vmem, vmem, hbm, hbm],
+        in_specs=[hbm] * 10,
         out_specs=(vmem, vmem),
         scratch_shapes=[
+            pltpu.VMEM(keys.shape, BF16), pltpu.VMEM(values.shape, BF16), pltpu.VMEM((1, half), F32),
+            pltpu.VMEM((TOPK, tokens), jnp.int32), pltpu.VMEM((TOPK, tokens), F32),
             pltpu.VMEM((tokens * heads, size), BF16),
             pltpu.VMEM((tokens, half), BF16),
             pltpu.VMEM((n, 2 * tokens, size), BF16),
             pltpu.VMEM((2, HALF_Z, 2, depth, wide), BF16),
             pltpu.VMEM((tokens * heads, size), F32),
-            pltpu.VMEM((tokens, heads * size), BF16),
-            pltpu.VMEM((3, 2, HALF_Z // 2, tokens, 2 * depth), BF16),
-            pltpu.VMEM((heads * size, 2 * depth), jnp.int32),
+            pltpu.VMEM((2, tokens, heads * size // 2), BF16),
+            pltpu.VMEM((3, 2, 2, HALF_Z // PLANE, tokens, PLANE * depth // 2), BF16),
+            pltpu.VMEM((heads * size // 2, PLANE * depth // 2), jnp.int32),
             pltpu.VMEM((2, 2 * tokens, wide), F32),
             pltpu.VMEM((2, tokens, wide), BF16),
             pltpu.VMEM((2, tokens, wide), BF16),
@@ -621,23 +687,25 @@
             pltpu.VMEM((tokens, 128), F32),
             pltpu.VMEM((tokens, half), F32),
             pltpu.VMEM((rows * blocks, 128), F32),
-            pltpu.VMEM((rows, half), BF16),
+            pltpu.VMEM((2, rows // 2, half), BF16),
             pltpu.VMEM(box, BF16), pltpu.VMEM(box, BF16), pltpu.VMEM(box, BF16), pltpu.VMEM(box, BF16),
-            pltpu.VMEM((units // width, 2, rows, width), BF16),
-            pltpu.VMEM((units // width, 2, rows, width), BF16),
-            pltpu.VMEM((rows, units), BF16),
+            pltpu.VMEM((2, units // width, 2, rows // 2, width), BF16),
+            pltpu.VMEM((2, units // width, 2, rows // 2, width), BF16),
+            pltpu.VMEM((rows // 2, units), BF16),
+            pltpu.VMEM((2, rows, tokens), BF16),
+            pltpu.VMEM((tokens, half), BF16),
             dma((15,)), dma((n,)), dma((2, 2)), dma((2,)), dma((2, 2)), dma((2,)),
-            dma((4, 2, 2)), dma((HALF_Z, 2, 2)), dma((2,)), dma((3,)), dma((3,)), dma((2,)), dma((2,)),
-            dma((2,)), dma((units // width,)), dma((units // width,)),
-            dma((n,)), dma((n,)), dma((n,)), dma((n,)), dma((6,)),
+            dma((4, 2, 2)), dma((HALF_Z, 2, 2)), dma((2,)), dma((3, 2)), dma((3, 2)), dma((2,)), dma((2,)),
+            dma((2,)), dma((2, units // width)), dma((2, units // width)),
+            dma((n,)), dma((n,)), dma((n,)), dma((n,)), dma((11,)),
         ],
         compiler_params=pltpu.CompilerParams(
             collective_id=0, has_side_effects=True, vmem_limit_bytes=56 * 2**20
         ),
         name="layer",
     )(
-        queries.reshape(tokens * heads, size), keys.reshape(tokens, -1), values.reshape(tokens, -1),
-        w_out.reshape(depth, 2 * half), resid, gain.reshape(1, half), expert_ids, gate_scores,
+        queries.reshape(tokens * heads, size), keys, values,
+        w_out.reshape(depth, 2 * half), resid, gain.reshape(1, half), expert_ids.T, gate_scores.T,
         w_gate_up[0], w_down[0],
     )
     return (context.reshape(tokens, heads, size), mixed)

time: 134 us -> 130 us (0.970); the launches traced: 132 us -> 130 us
  local copies, waits for them, and re-layouts: 8.11 us -> 3.75 us
  Pallas kernels: 123 us -> 126 us
    unnamed x4 -> x2, local copies, waits for them, and re-layouts: 6.57 us -> 3.75 us
    pallas_call x1, Pallas kernels: 123 us -> 126 us  [fast_body(): pl.pallas_call(layer_kernel, out_shape=(jax.ShapeDtypeStruct((tokens * he...]
    reshape x1 -> x0, local copies, waits for them, and re-layouts: 1.54 us -> none  [fast_body(): values.reshape(tokens, -1)]
where the time goes in v3:
time: 130 us
  Pallas kernels  126 us (97%)
  local copies, waits for them, and re-layouts  3.75 us (3%)
    pallas_call x1, Pallas kernels, fast_body(): pl.pallas_call(layer_kernel, out_shape=(jax.ShapeDtypeStruct((tokens * he...  126 us
    unnamed x2, local copies, waits for them, and re-layouts  3.75 us

profile of v3, /device:TPU:1, one launch (start us, length us, event | category | flops | bytes accessed | tf_op | source)
XLA Modules:
  0.0 130.1 jit_solution(7727864733562041008)
XLA Ops:
  0.6 125.7 %layer.1 = (bf16[2048,128]{1,0:T(8,128)(2,1)}, bf16[128,2048]{1,0:T(8,128)(2,1)}) custom-call(bf16[2048,128]{1,0:T(8,128)(2,1)} %bitcast.11, bf16[128,2,128]{2,1,0:T(2,128)(2,1)} %key_hbm.1, bf16[128,2,128]{2,1,0:T(2,128)(2,1)} %value_hbm.1, bf16[128,4096]{1,0:T(8,128)(2,1)} %bitcast.10, bf16[128,2048]{1,0:T(8,128)(2,1)} %resid_hbm.1, f32[1,2048]{1,0:T(1,128)} %bitcast.13, ...), custom_call_target="tpu_custom_call" | custom-call | tf_op jit(solution)/shard_map/layer/pallas_call | solution.py:661
  126.3 1.9 %copy.14 = bf16[128,16,128]{2,1,0:T(8,128)(2,1)} copy(bf16[128,16,128]{2,1,0:T(8,128)(2,1)} %bitcast.12) | data formatting | bytes 1048576
  128.2 1.9 %copy.15 = bf16[128,2048]{1,0:T(8,128)(2,1)} copy(bf16[128,2048]{1,0:T(8,128)(2,1)} %get-tuple-element.9) | data formatting | bytes 1048576

commit v4 on v3

--- a/solution.py
+++ b/solution.py
@@ -158,7 +158,7 @@
     q_hbm, key_hbm, value_hbm, w_hbm, resid_hbm, gain_hbm, ids_hbm, gate_hbm, gu_hbm, down_hbm,
     ctx_ref, mixed_ref,
     key_ref, value_ref, gain_ref, ids_ref, gate_ref, q_in, resid, kvbuf, wbuf, rows32, ctx2d, ctxbuf, target, acc, part_out, part_in,
-    gu_raw, gu, down, squares, peer_squares, hidden_buf, stage, two, outbox, inbox, backbox, endbox,
+    gu, down, squares, peer_squares, hidden_buf, stage, two, outbox, inbox, backbox, endbox,
     parts, peer_parts, act, mixes, normed_buf,
     kv_send, kv_recv, own_z, fwd_z, own_y, fwd_y, w_sib, w_recv, x_send, c_send, c_recv, h_send, h_recv,
     sq_sem, p_send, p_recv, a_send, a_recv, b_send, b_recv, local_sem,
@@ -208,7 +208,7 @@
 
     load_q = pltpu.make_async_copy(q_hbm, q_in, local_sem.at[2])
     load_resid = pltpu.make_async_copy(resid_hbm, resid, local_sem.at[3])
-    load_gu = pltpu.make_async_copy(gu_hbm, gu_raw, local_sem.at[4])
+    load_gu = pltpu.make_async_copy(gu_hbm, gu, local_sem.at[4])
     load_down = pltpu.make_async_copy(down_hbm, down, local_sem.at[5])
     small = [
         pltpu.make_async_copy(source, held, local_sem.at[6 + i])
@@ -387,18 +387,6 @@
         w_copy(block_of(1, 0, 0), 1, g, w_sib.at[1, 1, g], sibling).start()
 
     units = down.shape[0]
-    unpack_rows = 128
-
-    def unpack(first, count):
-        @pl.loop(first, first + count)
-        def _(i):
-            at = pl.ds(pl.multiple_of(i * unpack_rows, unpack_rows), unpack_rows)
-            gu[at, :units] = gu_raw[at, 0, :]
-            gu[at, units:] = gu_raw[at, 1, :]
-
-    n_unpack = half // unpack_rows
-    load_gu.wait()
-    unpack(0, n_unpack // 4)
     pass_on(1)
 
     def relay_far(f):
@@ -409,7 +397,6 @@
             w_copy(block_of(1, 1, 0), f, g, w_sib.at[3, f, g], sibling).start()
 
     relay_far(0)
-    unpack(n_unpack // 4, n_unpack // 4)
     ctx_ref[...] = rows32[...].astype(BF16)
     acc[...] = jnp.zeros_like(acc)
     for hh in range(2):
@@ -449,7 +436,7 @@
     relay_far(1)
     project(1)
     load_resid.wait()
-    unpack(n_unpack // 2, n_unpack // 4)
+    load_gu.wait()
 
     for copy in small[2:]:
         copy.wait()
@@ -551,7 +538,6 @@
 
     far_first(lambda to: a_copy(to).start())
     inbox[c] = outbox[c]
-    unpack(3 * (n_unpack // 4), n_unpack // 4)
     width = parts.shape[4]
 
     def p_copy(t, m):
@@ -641,6 +627,15 @@
     for t in range(2):
         for m in range(n_parts):
             p_copy(t, m).wait_send()
+
+
+def hand_over(context_in, mixed_in, context_out, mixed_out, sem):
+    first = pltpu.make_async_copy(context_in, context_out, sem.at[0])
+    second = pltpu.make_async_copy(mixed_in, mixed_out, sem.at[1])
+    first.start()
+    second.start()
+    first.wait()
+    second.wait()
 
 
 def fast_body(queries, keys, values, resid, gain, expert_ids, gate_scores, w_gate_up, w_down, w_out):
@@ -680,7 +675,6 @@
             pltpu.VMEM((2, 2 * tokens, wide), F32),
             pltpu.VMEM((2, tokens, wide), BF16),
             pltpu.VMEM((2, tokens, wide), BF16),
-            pltpu.VMEM((half, 2, units), BF16),
             pltpu.VMEM((half, 2 * units), BF16),
             pltpu.VMEM((units, half), BF16),
             pltpu.VMEM((tokens, 128), F32),
@@ -706,8 +700,20 @@
     )(
         queries.reshape(tokens * heads, size), keys, values,
         w_out.reshape(depth, 2 * half), resid, gain.reshape(1, half), expert_ids.T, gate_scores.T,
-        w_gate_up[0], w_down[0],
+        w_gate_up[0].reshape(half, 2 * units), w_down[0],
     )
+    context, mixed = pl.pallas_call(
+        hand_over,
+        out_shape=(
+            jax.ShapeDtypeStruct((tokens * heads, size), BF16),
+            jax.ShapeDtypeStruct((tokens, half), BF16),
+        ),
+        in_specs=[hbm, hbm],
+        out_specs=(hbm, hbm),
+        scratch_shapes=[dma((2,))],
+        compiler_params=pltpu.CompilerParams(vmem_limit_bytes=56 * 2**20),
+        name="hand_over",
+    )(context, mixed)
     return (context.reshape(tokens, heads, size), mixed)
 
 

time: 130 us -> 162 us (1.25)
  Pallas kernels: 126 us -> 155 us
  local copies, waits for them, and re-layouts: 3.75 us -> 6.79 us
    pallas_call x0 -> x1, Pallas kernels: none -> 32.9 us  [fast_body(): pl.pallas_call(hand_over, out_shape=(jax.ShapeDtypeStruct((tokens * heads...]
    pallas_call x1, Pallas kernels: 126 us -> 122 us  [fast_body(): pl.pallas_call(layer_kernel, out_shape=(jax.ShapeDtypeStruct((tokens * he...]
    unnamed x2 -> x1, local copies, waits for them, and re-layouts: 3.75 us -> 6.79 us
where the time goes in v4:
time: 162 us
  Pallas kernels  155 us (96%)
  local copies, waits for them, and re-layouts  6.79 us (4%)
    pallas_call x1, Pallas kernels, fast_body(): pl.pallas_call(layer_kernel, out_shape=(jax.ShapeDtypeStruct((tokens * he...  122 us
    pallas_call x1, Pallas kernels, fast_body(): pl.pallas_call(hand_over, out_shape=(jax.ShapeDtypeStruct((tokens * heads...  32.9 us
    unnamed x1, local copies, waits for them, and re-layouts  6.79 us

profile of v4, /device:TPU:1, one launch (start us, length us, event | category | flops | bytes accessed | tf_op | source)
XLA Modules:
  0.0 162.0 jit_solution(462255863578355596)
XLA Ops:
  0.6 6.8 %copy.12 = bf16[256,8,2,768]{3,1,2,0:T(8,128)(2,1)} copy(bf16[256,8,2,768]{3,2,1,0:T(2,128)(2,1)} %bitcast.11) | data formatting | bytes 12582912
  7.4 121.7 %layer.1 = (bf16[2048,128]{1,0:T(8,128)(2,1)}, bf16[128,2048]{1,0:T(8,128)(2,1)}) custom-call(bf16[2048,128]{1,0:T(8,128)(2,1)} %bitcast.14, bf16[128,2,128]{2,1,0:T(2,128)(2,1)} %key_hbm.1, bf16[128,2,128]{2,1,0:T(2,128)(2,1)} %value_hbm.1, bf16[128,4096]{1,0:T(8,128)(2,1)} %bitcast.13, bf16[128,2048]{1,0:T(8,128)(2,1)} %resid_hbm.1, f32[1,2048]{1,0:T(1,128)} %bitcast.15, ...), custom_call_target="tpu_custom_call" | custom-call | tf_op jit(solution)/shard_map/layer/pallas_call | solution.py:656
  129.2 32.9 %hand_over.1 = (bf16[2048,128]{1,0:T(8,128)(2,1)}, bf16[128,2048]{1,0:T(8,128)(2,1)}) custom-call(bf16[2048,128]{1,0:T(8,128)(2,1)} %get-tuple-element.6.context_in, bf16[128,2048]{1,0:T(8,128)(2,1)} %get-tuple-element.7.mixed_in), custom_call_target="tpu_custom_call" | custom-call | tf_op jit(solution)/shard_map/hand_over/pallas_call | solution.py:705

commit v5 on v3

--- a/solution.py
+++ b/solution.py
@@ -157,7 +157,7 @@
 def layer_kernel(
     q_hbm, key_hbm, value_hbm, w_hbm, resid_hbm, gain_hbm, ids_hbm, gate_hbm, gu_hbm, down_hbm,
     ctx_ref, mixed_ref,
-    key_ref, value_ref, gain_ref, ids_ref, gate_ref, q_in, resid, kvbuf, wbuf, rows32, ctx2d, ctxbuf, target, acc, part_out, part_in,
+    key_ref, value_ref, gain_ref, ids_ref, gate_ref, w_held, q_in, resid, kvbuf, wbuf, rows32, ctx2d, ctxbuf, target, acc, part_out, part_in,
     gu_raw, gu, down, squares, peer_squares, hidden_buf, stage, two, outbox, inbox, backbox, endbox,
     parts, peer_parts, act, mixes, normed_buf,
     kv_send, kv_recv, own_z, fwd_z, own_y, fwd_y, w_sib, w_recv, x_send, c_send, c_recv, h_send, h_recv,
@@ -221,6 +221,8 @@
     ]
     for copy in small:
         copy.start()
+    load_w = pltpu.make_async_copy(w_hbm, w_held, local_sem.at[11])
+    load_w.start()
     own_load(0).start()
     own_load(1).start()
     load_q.start()
@@ -252,7 +254,7 @@
 
     def swap(f):
         return pltpu.make_async_remote_copy(
-            src_ref=w_hbm.at[:, pl.ds(pl.multiple_of((1 - e) * half + f * wide, wide), wide)],
+            src_ref=w_held.at[:, pl.ds(pl.multiple_of((1 - e) * half + f * wide, wide), wide)],
             dst_ref=wbuf.at[f, mine, e], send_sem=x_send.at[f], recv_sem=w_recv.at[mine, f, e],
             device_id=(c, 1 - e), device_id_type=MESH,
         )
@@ -270,6 +272,7 @@
         kv_copy(c, step - 1, ((z + step) % N_Z) * PLANE + plane).start()
     kv_copy(c, 3, y_peer).start()
     kv_copy(c, 7, sibling).start()
+    load_w.wait()
     swap(0).start()
     swap(1).start()
     load_q.wait()
@@ -281,16 +284,16 @@
         kv_copy(block, 7 + step, sibling).start()
     own_load(0).wait()
     send_own(0, 0)
+    for step in range(N_Z):
+        block = ((z + step) % N_Z) * PLANE + (1 - y) * 2 + k
+        kv_copy(block, 0, sibling).wait_recv()
+        kv_copy(block, 11 + step, sibling).start()
     wait_block(mine, 0, group_of(1))
     send_own(0, 1)
     own_load(1).wait()
     send_own(1, 0)
     wait_block(mine, 1, group_of(1))
     send_own(1, 1)
-    for step in range(N_Z):
-        block = ((z + step) % N_Z) * PLANE + (1 - y) * 2 + k
-        kv_copy(block, 0, sibling).wait_recv()
-        kv_copy(block, 11 + step, sibling).start()
     depth_part = depth // 2
     row = lax.broadcasted_iota(jnp.int32, target.shape, 0)
     col = lax.broadcasted_iota(jnp.int32, target.shape, 1)
@@ -669,6 +672,7 @@
         scratch_shapes=[
             pltpu.VMEM(keys.shape, BF16), pltpu.VMEM(values.shape, BF16), pltpu.VMEM((1, half), F32),
             pltpu.VMEM((TOPK, tokens), jnp.int32), pltpu.VMEM((TOPK, tokens), F32),
+            pltpu.VMEM((depth, 2 * half), BF16),
             pltpu.VMEM((tokens * heads, size), BF16),
             pltpu.VMEM((tokens, half), BF16),
             pltpu.VMEM((n, 2 * tokens, size), BF16),
@@ -697,7 +701,7 @@
             dma((15,)), dma((n,)), dma((2, 2)), dma((2,)), dma((2, 2)), dma((2,)),
             dma((4, 2, 2)), dma((HALF_Z, 2, 2)), dma((2,)), dma((3, 2)), dma((3, 2)), dma((2,)), dma((2,)),
             dma((2,)), dma((2, units // width)), dma((2, units // width)),
-            dma((n,)), dma((n,)), dma((n,)), dma((n,)), dma((11,)),
+            dma((n,)), dma((n,)), dma((n,)), dma((n,)), dma((12,)),
         ],
         compiler_params=pltpu.CompilerParams(
             collective_id=0, has_side_effects=True, vmem_limit_bytes=56 * 2**20

time: 130 us -> 130 us (level)
  no operation moved by 1% of the time
where the time goes in v5:
time: 130 us
  Pallas kernels  126 us (97%)
  local copies, waits for them, and re-layouts  3.75 us (3%)
    pallas_call x1, Pallas kernels, fast_body(): pl.pallas_call(layer_kernel, out_shape=(jax.ShapeDtypeStruct((tokens * he...  126 us
    unnamed x2, local copies, waits for them, and re-layouts  3.75 us

profile of v5, /device:TPU:1, one launch (start us, length us, event | category | flops | bytes accessed | tf_op | source)
XLA Modules:
  0.0 130.1 jit_solution(15934331783286164643)
XLA Ops:
  0.6 125.7 %layer.1 = (bf16[2048,128]{1,0:T(8,128)(2,1)}, bf16[128,2048]{1,0:T(8,128)(2,1)}) custom-call(bf16[2048,128]{1,0:T(8,128)(2,1)} %bitcast.11, bf16[128,2,128]{2,1,0:T(2,128)(2,1)} %key_hbm.1, bf16[128,2,128]{2,1,0:T(2,128)(2,1)} %value_hbm.1, bf16[128,4096]{1,0:T(8,128)(2,1)} %bitcast.10, bf16[128,2048]{1,0:T(8,128)(2,1)} %resid_hbm.1, f32[1,2048]{1,0:T(1,128)} %bitcast.13, ...), custom_call_target="tpu_custom_call" | custom-call | tf_op jit(solution)/shard_map/layer/pallas_call | solution.py:664
  126.3 1.9 %copy.14 = bf16[128,16,128]{2,1,0:T(8,128)(2,1)} copy(bf16[128,16,128]{2,1,0:T(8,128)(2,1)} %bitcast.12) | data formatting | bytes 1048576
  128.2 1.9 %copy.15 = bf16[128,2048]{1,0:T(8,128)(2,1)} copy(bf16[128,2048]{1,0:T(8,128)(2,1)} %get-tuple-element.9) | data formatting | bytes 1048576
